TPU v7x, 256 devices: a whole 4x4x8 slice. The times are simulated.
256 devices in a mesh: ctx: 32 (over z, y_hi, core), doc: 8 (over x, y_lo).
Axes of the slice: x: 4, y: 4 (y_hi: 2, y_lo: 2; y = y_hi * 2 + y_lo), z: 8, core: 2. Of those that a mesh axis runs over, the one named last changes fastest.
Arguments:
- activations: float32 [8, 8192, 1024], P('doc', 'ctx'), may hold values from -60 to 60
- queries: float32 [8, 8192, 512], P('doc', 'ctx'), may hold values from -8 to 8
- d_out: float32 [8, 8192, 512], P('doc', 'ctx'), may hold values from -6 to 6
- w_kv: float32 [1024, 1024], replicated, may hold values from -1 to 1
- partner: int32 [8, 32], P('doc', 'ctx'), may hold values from 0 to 31, as said below
- block_mask: int32 [8, 32, 4, 4], P('doc', 'ctx'), may hold values from 0 to 1, as said below
Outputs:
- attended: float32 [8, 8192, 512], P('doc', 'ctx')
- grad_w_kv: float32 [1024, 1024], P('ctx', 'doc')
Inputs may be any that keep to these rules, and one draw needn't show every extreme that they name: partner[d, i] = i XOR s_d, where s_d of 1 to 31 is the same for all shards of document d, so shards are matched in pairs. `block_mask`: any 0/1 values; a shard's mask may be all zero or all one, and partners' masks are independent.
All inputs are finite; a program needn't handle non-finite values.
Results may differ from a plain program's by a relative error of at most 0.0003.
Values sent between devices are 32-bit elements; how exact they have to be, the bound alone decides.
A program may use at most 64 MiB of HBM per device.

v0:
```python
import math

import jax
import jax.numpy as jnp
from jax import lax
from jax.sharding import PartitionSpec as P

HEAD = 64


highest = lax.Precision.HIGHEST
masked_score = -1e30


def from_partner(value, axis, bit):
    mask = 2**bit
    pairs = [(source, source ^ mask) for source in range(lax.axis_size(axis))]
    return lax.ppermute(value, axis, pairs)


def visible_keys(mask_blocks, count):
    block = count // mask_blocks.shape[0]
    partner_part = jnp.repeat(jnp.repeat(mask_blocks, block, axis=0), block, axis=1) == 1
    return jnp.concatenate([jnp.ones((count, count), jnp.bool_), partner_part], axis=1)


def attend_shard(query_rows, key_rows, value_rows, visible, cotangent):
    factor = 1.0 / math.sqrt(query_rows.shape[2])
    scores = jnp.einsum("qhd,khd->hqk", query_rows, key_rows, precision=highest) * factor
    scores = jnp.where(visible[None], scores, masked_score)
    maximum = jnp.max(scores, axis=2, keepdims=True)
    raised = jnp.exp(scores - maximum)
    totals = jnp.sum(raised, axis=2, keepdims=True)
    weights = raised / totals
    attended = jnp.einsum("hqk,khd->qhd", weights, value_rows, precision=highest)
    grad_weights = jnp.einsum("qhd,khd->hqk", cotangent, value_rows, precision=highest)
    row_dot = jnp.transpose(jnp.sum(cotangent * attended, axis=2))[:, :, None]
    grad_scores = weights * (grad_weights - row_dot)
    grad_keys = jnp.einsum("hqk,qhd->khd", grad_scores, query_rows, precision=highest) * factor
    grad_values = jnp.einsum("hqk,qhd->khd", weights, cotangent, precision=highest)
    return (attended, grad_keys, grad_values)


def contract_rows(left, right):
    return lax.dot_general(left, right, (((0,), (0,)), ((), ())), precision=highest)


def shards(activations, queries, d_out, w_kv, partner, block_mask):
    token_rows = activations[0]
    query_flat = queries[0]
    cotangent_flat = d_out[0]
    count = token_rows.shape[0]
    width = query_flat.shape[1]
    heads = width // HEAD
    offset = jnp.bitwise_xor(partner[0, 0], lax.axis_index("ctx"))
    digits = lax.axis_size("ctx").bit_length() - 1
    sequence = list(range(digits))
    own_pairs = jnp.dot(token_rows, w_kv, precision=highest)
    far_pairs = own_pairs
    for bit_index in sequence:
        moved = from_partner(far_pairs, "ctx", bit_index)
        far_pairs = jnp.where(jnp.right_shift(offset, bit_index) % 2 == 1, moved, far_pairs)
    joined = jnp.concatenate([own_pairs, far_pairs], axis=0)
    key_rows = joined[:, :width].reshape(2 * count, heads, HEAD)
    value_rows = joined[:, width:].reshape(2 * count, heads, HEAD)
    visible = visible_keys(block_mask[0, 0], count)
    attended, grad_keys, grad_values = attend_shard(
        query_flat.reshape(count, heads, HEAD),
        key_rows,
        value_rows,
        visible,
        cotangent_flat.reshape(count, heads, HEAD),
    )
    grad_pairs = jnp.concatenate(
        [grad_keys.reshape(2 * count, width), grad_values.reshape(2 * count, width)], axis=1
    )
    own_grads = grad_pairs[:count]
    far_grads = grad_pairs[count:]
    factor = 1.0 / math.sqrt(count * lax.axis_size("ctx") * lax.axis_size("doc"))
    returned = far_grads
    for bit_index in sequence:
        moved = from_partner(returned, "ctx", bit_index)
        returned = jnp.where(jnp.right_shift(offset, bit_index) % 2 == 1, moved, returned)
    term = contract_rows(token_rows, own_grads + returned)
    term = term * factor
    partial_sum = lax.psum_scatter(term, "ctx", scatter_dimension=0, tiled=True)
    gradient = lax.psum_scatter(partial_sum, "doc", scatter_dimension=1, tiled=True)
    return (attended.reshape(1, count, width), gradient)


def solution(mesh):
    placed = (
        P("doc", "ctx", None),
        P("doc", "ctx", None),
        P("doc", "ctx", None),
        P(),
        P("doc", "ctx"),
        P("doc", "ctx", None, None),
    )
    return jax.shard_map(
        shards,
        mesh=mesh,
        in_specs=placed,
        out_specs=(P("doc", "ctx", None), P("ctx", "doc")),
        check_vma=False,
    )
```

profile of v0, /device:TPU:2, one launch (start us, length us, event | category | flops | bytes accessed | tf_op | source)
XLA Modules:
  0.0 543.7 jit_solution(1336397255299647454)
XLA Ops:
  8.4 5.7 %fusion.12 = f32[256,1024]{1,0:T(8,128)S(1)} fusion(f32[1024,1024]{1,0:T(8,128)} %param.9, f32[1,256,1024]{2,1,0:T(8,128)S(1)} %copy-done), kind=kOutput, calls=%fused_computation.21 | convolution fusion | flops 3221225472 | bytes 6291456 | tf_op jit(solution)/shard_map/dot_general | solution.py:58
  14.9 2.1 collective-permute-done
  18.4 3.3 collective-permute-start.1
  21.6 23.6 %collective-permute-done.1 = f32[256,1024]{1,0:T(8,128)} collective-permute-done((f32[256,1024]{1,0:T(8,128)S(1)}, f32[256,1024]{1,0:T(8,128)}, u32[]{:S(2)}, u32[]{:S(2)}) %collective-permute-start.1) | collective-permute-done | bytes 1048608 | tf_op jit(solution)/shard_map/ppermute | solution.py:18
  46.7 2.0 collective-permute-start.2
  48.7 22.7 %collective-permute-done.2 = f32[256,1024]{1,0:T(8,128)} collective-permute-done((f32[256,1024]{1,0:T(8,128)S(1)}, f32[256,1024]{1,0:T(8,128)}, u32[]{:S(2)}, u32[]{:S(2)}) %collective-permute-start.2) | collective-permute-done | bytes 1048608 | tf_op jit(solution)/shard_map/ppermute | solution.py:18
  72.8 3.4 collective-permute-start.3
  76.1 44.5 %collective-permute-done.3 = f32[256,1024]{1,0:T(8,128)} collective-permute-done((f32[256,1024]{1,0:T(8,128)S(1)}, f32[256,1024]{1,0:T(8,128)}, u32[]{:S(2)}, u32[]{:S(2)}) %collective-permute-start.3) | collective-permute-done | bytes 1048608 | tf_op jit(solution)/shard_map/ppermute | solution.py:18
  122.0 6.5 %collective-permute-start.4 = (f32[256,1024]{1,0:T(8,128)S(1)}, f32[256,1024]{1,0:T(8,128)}, u32[]{:S(2)}, u32[]{:S(2)}) collective-permute-start(f32[256,1024]{1,0:T(8,128)S(1)} %broadcast_select_fusion.7), channel_id=1, source_target_pairs={{0,128},{8,136},{16,144},{24,152},{32,160},{40,168},{48,176},{56,1... | collective-permute-start | bytes 3145736 | tf_op jit(solution)/shard_map/ppermute | solution.py:18
  128.4 2.0 copy.38
  130.8 2.1 copy.36
  132.9 41.3 %collective-permute-done.4 = f32[256,1024]{1,0:T(8,128)} collective-permute-done((f32[256,1024]{1,0:T(8,128)S(1)}, f32[256,1024]{1,0:T(8,128)}, u32[]{:S(2)}, u32[]{:S(2)}) %collective-permute-start.4) | collective-permute-done | bytes 1048608 | tf_op jit(solution)/shard_map/ppermute | solution.py:18
  175.5 1.6 copy.33
  178.4 5.4 fusion.4
  184.6 3.6 fusion.23
  188.3 4.6 fusion.15
  192.9 6.1 %fusion.18 = f32[8,512,64]{1,2,0:T(8,128)} fusion(f32[256,8,64]{0,2,1:T(8,128)S(1)} %bitcast.67, f32[8,512,256]{2,1,0:T(8,128)S(1)} %get-tuple-element.11, f32[8,256]{1,0:T(8,128)S(1)} %fusion.3, f32[8,256]{1,0:T(8,128)S(1)} %get-tuple-element.10, pred[256,512]{0,1:T(8,128)(4,1)S(1)} %concatenate.10), kind=kOutput, calls=%fused_computation.38 | convolution fusion | flops 809500672 | bytes 5914624 | tf_op jit(solution)/shard_map/hqk,qhd->khd/dot_general | solution.py:40
  199.0 5.5 %fusion.6 = f32[8,512,64]{1,2,0:T(8,128)S(1)} fusion(f32[256,8,64]{0,2,1:T(8,128)S(1)} %bitcast.64, f32[8,512,256]{2,1,0:T(8,128)S(1)} %fusion.23, f32[8,256]{1,0:T(8,128)S(1)} %bitcast.72, f32[8,512,256]{2,1,0:T(8,128)S(1)} %get-tuple-element.11, f32[8,256]{1,0:T(8,128)S(1)} %fusion.3, f32[8,256]{1,0:T(8,128)S(1)} %get-tuple-element.10, ...), kind=kOutput, calls=%fused_computation.14 | convolution fusion | flops 811859968 | bytes 10117120 | tf_op jit(solution)/shard_map/hqk,qhd->khd/dot_general | solution.py:39
  204.8 1.6 copy.42
  206.5 2.6 collective-permute-done.5
  209.3 3.3 collective-permute-start.6
  212.6 23.5 %collective-permute-done.6 = f32[256,1024]{1,0:T(8,128)S(1)} collective-permute-done((f32[256,1024]{1,0:T(8,128)S(1)}, f32[256,1024]{1,0:T(8,128)S(1)}, u32[]{:S(2)}, u32[]{:S(2)}) %collective-permute-start.6) | collective-permute-done | bytes 1048608 | tf_op jit(solution)/shard_map/ppermute | solution.py:18
  236.7 24.4 %collective-permute-done.7 = f32[256,1024]{1,0:T(8,128)S(1)} collective-permute-done((f32[256,1024]{1,0:T(8,128)S(1)}, f32[256,1024]{1,0:T(8,128)S(1)}, u32[]{:S(2)}, u32[]{:S(2)}) %collective-permute-start.7) | collective-permute-done | bytes 1048608 | tf_op jit(solution)/shard_map/ppermute | solution.py:18
  261.2 2.1 collective-permute-start.8
  263.3 44.9 %collective-permute-done.8 = f32[256,1024]{1,0:T(8,128)S(1)} collective-permute-done((f32[256,1024]{1,0:T(8,128)S(1)}, f32[256,1024]{1,0:T(8,128)S(1)}, u32[]{:S(2)}, u32[]{:S(2)}) %collective-permute-start.8) | collective-permute-done | bytes 1048608 | tf_op jit(solution)/shard_map/ppermute | solution.py:18
  308.3 2.8 collective-permute-start.9
  311.0 47.7 %collective-permute-done.9 = f32[256,1024]{1,0:T(8,128)S(1)} collective-permute-done((f32[256,1024]{1,0:T(8,128)S(1)}, f32[256,1024]{1,0:T(8,128)S(1)}, u32[]{:S(2)}, u32[]{:S(2)}) %collective-permute-start.9) | collective-permute-done | bytes 1048608 | tf_op jit(solution)/shard_map/ppermute | solution.py:18
  358.8 5.3 multiply_bitcast_fusion
  364.1 5.4 copy.48
  369.5 127.1 %reduce-scatter.7.cloned.1.call-done = f32[32,1024]{1,0:T(8,128)} async-done(((f32[1024,1024]{1,0:T(8,128)}), f32[32,1024]{1,0:T(8,128)}) %reduce-scatter.7.cloned.1.call-update) | async-done | bytes 131088
  496.7 1.9 copy.49
  499.6 35.7 %reduce-scatter.5.cloned.1.call-done = f32[32,128]{0,1:T(8,128)} async-done(((f32[32,1024]{0,1:T(8,128)}), f32[32,128]{0,1:T(8,128)}) %reduce-scatter.5.cloned.1.call-update) | async-done | bytes 16400 | tf_op jit(solution)/shard_map/reduce_scatter | solution.py:87
  (45 shorter events, 14.8 us)
Async XLA Ops:
  7.2 1.2 copy-start
  7.2 489.5 %reduce-scatter.7.cloned.1.call-start = ((), (), s32[]{:S(2)}) async-start(), calls=%async_computation.3 | async-start | bytes 4325376
  14.1 2.9 collective-permute-start
  18.4 3.3 copy-start.3
  18.4 26.9 %collective-permute-start.1 = (f32[256,1024]{1,0:T(8,128)S(1)}, f32[256,1024]{1,0:T(8,128)}, u32[]{:S(2)}, u32[]{:S(2)}) collective-permute-start(f32[256,1024]{1,0:T(8,128)S(1)} %broadcast_select_fusion.1), channel_id=1, source_target_pairs={{0,16},{8,24},{16,0},{24,8},{32,48},{40,56},{48,32},{56,40},{64,80... | collective-permute-start | bytes 3145736 | tf_op jit(solution)/shard_map/ppermute | solution.py:18
  46.6 2.0 copy-start.2
  46.6 83.8 %copy-start.7 = (s32[1,1,4,4]{3,2,1,0:T(4,128)S(1)}, s32[1,1,4,4]{3,2,1,0:T(4,128)}, u32[]{:S(2)}) copy-start(s32[1,1,4,4]{3,2,1,0:T(4,128)} %param.11) | copy-start | bytes 196
  46.7 24.7 %collective-permute-start.2 = (f32[256,1024]{1,0:T(8,128)S(1)}, f32[256,1024]{1,0:T(8,128)}, u32[]{:S(2)}, u32[]{:S(2)}) collective-permute-start(f32[256,1024]{1,0:T(8,128)S(1)} %broadcast_select_fusion.3), channel_id=1, source_target_pairs={{0,32},{8,40},{16,48},{24,56},{32,0},{40,8},{48,16},{56,24},{64,96... | collective-permute-start | bytes 3145736 | tf_op jit(solution)/shard_map/ppermute | solution.py:18
  72.8 3.4 copy-start.1
  72.8 47.8 %collective-permute-start.3 = (f32[256,1024]{1,0:T(8,128)S(1)}, f32[256,1024]{1,0:T(8,128)}, u32[]{:S(2)}, u32[]{:S(2)}) collective-permute-start(f32[256,1024]{1,0:T(8,128)S(1)} %broadcast_select_fusion.5), channel_id=1, source_target_pairs={{0,64},{8,72},{16,80},{24,88},{32,96},{40,104},{48,112},{56,120},{... | collective-permute-start | bytes 3145736 | tf_op jit(solution)/shard_map/ppermute | solution.py:18
  122.0 52.2 %collective-permute-start.4 = (f32[256,1024]{1,0:T(8,128)S(1)}, f32[256,1024]{1,0:T(8,128)}, u32[]{:S(2)}, u32[]{:S(2)}) collective-permute-start(f32[256,1024]{1,0:T(8,128)S(1)} %broadcast_select_fusion.7), channel_id=1, source_target_pairs={{0,128},{8,136},{16,144},{24,152},{32,160},{40,168},{48,176},{56,1... | collective-permute-start | bytes 3145736 | tf_op jit(solution)/shard_map/ppermute | solution.py:18
  178.4 6.2 %copy-start.5 = (f32[1,256,512]{1,2,0:T(8,128)S(1)}, f32[1,256,512]{1,2,0:T(8,128)}, u32[]{:S(2)}) copy-start(f32[1,256,512]{1,2,0:T(8,128)} %copy.38) | copy-start | bytes 1572868
  192.9 6.1 %copy-start.4 = (f32[1,256,512]{1,2,0:T(8,128)S(1)}, f32[1,256,512]{1,2,0:T(8,128)}, u32[]{:S(2)}) copy-start(f32[1,256,512]{1,2,0:T(8,128)} %copy.36) | copy-start | bytes 1572868
  206.4 2.7 collective-permute-start.5
  209.3 26.8 %collective-permute-start.6 = (f32[256,1024]{1,0:T(8,128)S(1)}, f32[256,1024]{1,0:T(8,128)S(1)}, u32[]{:S(2)}, u32[]{:S(2)}) collective-permute-start(f32[256,1024]{1,0:T(8,128)S(1)} %broadcast_select_fusion), channel_id=1, source_target_pairs={{0,16},{8,24},{16,0},{24,8},{32,48},{40,56},{48,32},{56,40},{64,80... | collective-permute-start | bytes 3145736 | tf_op jit(solution)/shard_map/ppermute | solution.py:18
  236.3 24.7 %collective-permute-start.7 = (f32[256,1024]{1,0:T(8,128)S(1)}, f32[256,1024]{1,0:T(8,128)S(1)}, u32[]{:S(2)}, u32[]{:S(2)}) collective-permute-start(f32[256,1024]{1,0:T(8,128)S(1)} %broadcast_select_fusion.2), channel_id=1, source_target_pairs={{0,32},{8,40},{16,48},{24,56},{32,0},{40,8},{48,16},{56,24},{64,96... | collective-permute-start | bytes 3145736 | tf_op jit(solution)/shard_map/ppermute | solution.py:18
  261.2 46.9 %collective-permute-start.8 = (f32[256,1024]{1,0:T(8,128)S(1)}, f32[256,1024]{1,0:T(8,128)S(1)}, u32[]{:S(2)}, u32[]{:S(2)}) collective-permute-start(f32[256,1024]{1,0:T(8,128)S(1)} %broadcast_select_fusion.4), channel_id=1, source_target_pairs={{0,64},{8,72},{16,80},{24,88},{32,96},{40,104},{48,112},{56,120},{... | collective-permute-start | bytes 3145736 | tf_op jit(solution)/shard_map/ppermute | solution.py:18
  308.3 50.5 %collective-permute-start.9 = (f32[256,1024]{1,0:T(8,128)S(1)}, f32[256,1024]{1,0:T(8,128)S(1)}, u32[]{:S(2)}, u32[]{:S(2)}) collective-permute-start(f32[256,1024]{1,0:T(8,128)S(1)} %broadcast_select_fusion.6), channel_id=1, source_target_pairs={{0,128},{8,136},{16,144},{24,152},{32,160},{40,168},{48,176},{56,1... | collective-permute-start | bytes 3145736 | tf_op jit(solution)/shard_map/ppermute | solution.py:18
  369.5 129.2 %copy-start.6 = (f32[8,64,256]{2,1,0:T(8,128)S(1)}, f32[8,64,256]{2,1,0:T(8,128)}, u32[]{:S(2)}) copy-start(f32[8,64,256]{2,1,0:T(8,128)} %get-tuple-element.13) | copy-start | bytes 1572868
  369.5 165.9 %reduce-scatter.5.cloned.1.call-start = ((), (), s32[]{:S(2)}) async-start(), calls=%async_computation.2 | async-start | bytes 589824 | tf_op jit(solution)/shard_map/reduce_scatter | solution.py:87
Sparse Core Ops, SparseCore 0:
  369.6 127.0 reduce-scatter.6
  499.4 35.9 reduce-scatter.4
where the time goes:
time: 546 us; the launch traced here: 544 us
  waiting for transfers between devices  440 us (81%)
  matrix products  36.1 us (7%)
  starting transfers between devices  23.8 us (4%)
  local copies, waits for them, and re-layouts  20.2 us (4%)
  between operations  14.9 us (3%)
  other arithmetic  8.42 us (2%)
    ppermute x10, waiting for transfers between devices, from_partner(): return lax.ppermute(value, axis, pairs)  277 us
    unnamed x3, waiting for transfers between devices  127 us
    reduce_scatter x1, waiting for transfers between devices, shards(): lax.psum_scatter(partial_sum, 'doc', scatter_dimension=1, tiled=True)  35.7 us
    ppermute x10, starting transfers between devices, from_partner(): return lax.ppermute(value, axis, pairs)  23.8 us
    unnamed x22, local copies, waits for them, and re-layouts  15.1 us
  transfers between devices with their start and end apart: 12, of which 12 were waited for; matrix products, arithmetic and copies ran while one was open for 1% of the time, Pallas kernels for 0%

commit v1 on v0

v1 whole, which is shorter than its diff:
```python
import functools

import jax
import jax.numpy as jnp
from jax import lax
from jax.experimental import pallas as pl
from jax.experimental.pallas import tpu as pltpu
from jax.sharding import PartitionSpec as P

MESH = pl.DeviceIdType.MESH
F32, BF16 = jnp.float32, jnp.bfloat16
MASKED = -1e30
SLOTS = 16
CHUNKS = 8
MIB = 1024 * 1024


def split(x):
    hi = x.astype(BF16)
    return hi, (x - hi.astype(F32)).astype(BF16)


def nt_dot(a, b):
    return lax.dot_general(a, b, (((1,), (1,)), ((), ())), preferred_element_type=F32)


def nn_dot(a, b):
    return lax.dot_general(a, b, (((1,), (0,)), ((), ())), preferred_element_type=F32)


def remote(src, dst, send_sem, recv_sem, device):
    return pltpu.make_async_remote_copy(
        src_ref=src, dst_ref=dst, send_sem=send_sem, recv_sem=recv_sem,
        device_id=device, device_id_type=MESH,
    )


def exchange_kernel(partner_ref, act_ref, far_ref, core_in, base, y_in, z_out, z_in, dest,
                    core_s, core_r, y_s, y_r, z_s, z_r):
    me = lax.axis_index("ctx")
    z, rest = me // 4, me % 4
    core, yhi = me % 2, (me // 2) % 2
    core_dev = {"ctx": me + 1 - 2 * core}
    y_dev = {"ctx": me + 2 - 4 * yhi}
    right = {"ctx": ((z + 1) % 8) * 4 + rest}
    left = {"ctx": ((z + 7) % 8) * 4 + rest}
    z_dev = (right, left)
    barrier = pltpu.get_barrier_semaphore()
    for device in (core_dev, y_dev, right, left):
        pl.semaphore_signal(barrier, inc=1, device_id=device, device_id_type=MESH)
    pl.semaphore_wait(barrier, 4)

    offset = jnp.bitwise_xor(partner_ref[0, 0], me)
    flip_core = offset % 2 == 1
    flip_y = (offset // 2) % 2 == 1
    sz = offset // 4
    is4, is5 = sz == 4, sz == 5
    two = jnp.logical_or(sz == 2, sz == 6)
    three = jnp.logical_or(sz == 3, sz == 7)
    turned = sz >= 6
    is4_5 = jnp.logical_or(is4, is5)
    facing = (z, 7 - z)
    role = [jnp.where(turned, (zd + 2) % 4, zd % 4) for zd in facing]
    odd = [zd % 2 == 1 for zd in facing]

    rows = act_ref.shape[0] // CHUNKS
    order = (1, 0, 3, 2, 5, 4, 7, 6)
    core_cp, y_cp, z_cp = {}, {}, {}
    for j in order:
        core_cp[j] = remote(act_ref.at[pl.ds(j * rows, rows)], core_in.at[j], core_s.at[j], core_r.at[j], core_dev)
        core_cp[j].start()

    def own(j):
        if j % 2 == 1:
            return jnp.where(flip_y, y_in[j], base[j])
        return base[j]

    def ready(j):
        if j not in seen:
            seen.add(j)
            core_cp[j].wait_recv()
            base[j] = jnp.where(flip_core, core_in[j], act_ref[pl.ds(j * rows, rows)])
            if j % 2 == 1:
                y_cp[j] = remote(base.at[j], y_in.at[j], y_s.at[j], y_r.at[j], y_dev)
                y_cp[j].start()

    seen, arrived = set(), set()

    def want(j):
        ready(j)
        if j % 2 == 1 and j not in arrived:
            arrived.add(j)
            y_cp[j].wait_recv()

    for j in (1, 3, 5, 7, 0):
        ready(j)

    def got(t):
        for d in range(2):
            if (d, t) not in arrived:
                arrived.add((d, t))
                z_cp[d, t].wait_recv()

    for t in range(SLOTS):
        for d in range(2):
            if t < 4:
                want(t)
                want(2 * t + d)
                value = jnp.where(is4, own(2 * t + d), own(t))
            elif t < 8:
                got(t - 4)
                want(t)
                relay = jnp.logical_or(is4, jnp.logical_or(
                    jnp.logical_and(is5, jnp.logical_not(odd[d])), jnp.logical_and(three, role[d] == 1)))
                value = jnp.where(relay, z_in[d, t - 4], own(t))
            elif t < 12:
                got(t - 4)
                value = jnp.where(jnp.logical_or(is4_5, three), z_in[d, t - 4], z_in[d, t - 8])
            else:
                got(t - 4)
                late = jnp.logical_and(three, role[d] == 1)
                value = jnp.where(jnp.logical_or(is4_5, three), z_in[d, t - 4], z_in[d, t - 8])
                value = jnp.where(late, own(t - 8), value)
            z_out[d, t] = value
            z_cp[d, t] = remote(z_out.at[d, t], z_in.at[d, t], z_s.at[d, t], z_r.at[d, t], z_dev[d])
            z_cp[d, t].start()

    for k in range(CHUNKS):
        got(8 + k)
        got(12 + k // 2)
        value = own(k)
        for d in range(2):
            early = jnp.logical_and(sz == 1, odd[d])
            late = jnp.logical_or(
                jnp.logical_and(two, role[d] >= 2),
                jnp.logical_or(jnp.logical_and(three, role[d] == 3), jnp.logical_and(is5, jnp.logical_not(odd[d]))))
            near = jnp.logical_and(three, role[d] == 2)
            if k < 4:
                early = jnp.logical_or(early, near)
            else:
                late = jnp.logical_or(late, near)
            value = jnp.where(early, z_in[d, k], value)
            value = jnp.where(late, z_in[d, 8 + k], value)
        value = jnp.where(is4, z_in[k % 2, 12 + k // 2], value)
        if k % 2 == 0:
            dest[k] = value
            y_cp[k] = remote(dest.at[k], y_in.at[k], y_s.at[k], y_r.at[k], y_dev)
            y_cp[k].start()
        else:
            far_ref[pl.ds(k * rows, rows)] = value
    for k in range(0, CHUNKS, 2):
        y_cp[k].wait_recv()
        far_ref[pl.ds(k * rows, rows)] = jnp.where(flip_y, y_in[k], dest[k])
    for copies in (core_cp, y_cp, z_cp):
        for copy in copies.values():
            copy.wait_send()


def exchange(act, partner):
    count, depth = act.shape
    rows = count // CHUNKS
    chunk = lambda *lead: pltpu.VMEM(lead + (rows, depth), F32)
    dma = pltpu.SemaphoreType.DMA
    return pl.pallas_call(
        exchange_kernel,
        out_shape=jax.ShapeDtypeStruct((count, depth), F32),
        in_specs=[pl.BlockSpec(memory_space=pltpu.SMEM), pl.BlockSpec(memory_space=pltpu.VMEM)],
        out_specs=pl.BlockSpec(memory_space=pltpu.VMEM),
        scratch_shapes=[
            chunk(CHUNKS), chunk(CHUNKS), chunk(CHUNKS), chunk(2, SLOTS), chunk(2, SLOTS), chunk(CHUNKS),
            dma((CHUNKS,)), dma((CHUNKS,)), dma((CHUNKS,)), dma((CHUNKS,)), dma((2, SLOTS)), dma((2, SLOTS)),
        ],
        compiler_params=pltpu.CompilerParams(collective_id=0, has_side_effects=True, vmem_limit_bytes=32 * MIB),
    )(partner, act)


def attend(mask_ref, kv_hi, kv_lo, q_ref, d_ref, att_ref, g_hi, g_lo, s_ref, c_ref, w_hi, w_lo, t_hi, t_lo, pair):
    count, keys = q_ref.shape[0], kv_hi.shape[0]
    half = kv_hi.shape[1] // 2
    at = pl.ds(pl.multiple_of(pair * 128, 128), 128)
    at_v = pl.ds(pl.multiple_of(half + pair * 128, 128), 128)
    first = lax.broadcasted_iota(jnp.int32, (count, 128), 1) < 64
    k_h, k_l, v_h, v_l = kv_hi[:, at], kv_lo[:, at], kv_hi[:, at_v], kv_lo[:, at_v]

    def two_heads(x):
        return split(jnp.concatenate([jnp.where(first, x, 0.0), jnp.where(first, 0.0, x)], axis=0))

    q_h, q_l = two_heads(q_ref[:, at] * 0.125)
    d_h, d_l = two_heads(d_ref[:, at])
    cat = lambda *parts: jnp.concatenate(parts, axis=1)
    s_ref[...] = nt_dot(cat(k_h, k_h, k_l), cat(q_h, q_l, q_h))
    c_ref[...] = nt_dot(cat(v_h, v_h, v_l), cat(d_h, d_l, d_h))

    blocks, step = keys // 64, 64
    lanes = lax.broadcasted_iota(jnp.int32, (1, 2 * count), 1) % count // 64
    own_blocks = blocks // 2
    maximum = None
    for b in range(blocks):
        piece = s_ref[pl.ds(b * step, step), :]
        if b >= own_blocks:
            f = b - own_blocks
            seen = jnp.where(lanes == 0, mask_ref[0, f], jnp.where(lanes == 1, mask_ref[1, f], jnp.where(
                lanes == 2, mask_ref[2, f], mask_ref[3, f])))
            piece = jnp.where(seen == 1, piece, MASKED)
            s_ref[pl.ds(b * step, step), :] = piece
        top = jnp.max(piece, axis=0, keepdims=True)
        maximum = top if maximum is None else jnp.maximum(maximum, top)
    total, dots = 0.0, 0.0
    for b in range(blocks):
        rows = pl.ds(b * step, step)
        raised = jnp.exp(s_ref[rows, :] - maximum)
        s_ref[rows, :] = raised
        total = total + jnp.sum(raised, axis=0, keepdims=True)
        dots = dots + jnp.sum(raised * c_ref[rows, :], axis=0, keepdims=True)
    inverse = 1.0 / total
    row_dot = dots * inverse
    for b in range(blocks):
        rows = pl.ds(b * step, step)
        weight = s_ref[rows, :] * inverse
        w_hi[rows, :], w_lo[rows, :] = split(weight)
        t_hi[rows, :], t_lo[rows, :] = split(weight * (c_ref[rows, :] - row_dot))

    def grads(left_hi, left_lo, right_h, right_l):
        both = nn_dot(left_hi[...], cat(right_h, right_l))
        return both[:, :128] + both[:, 128:] + nn_dot(left_lo[...], right_h)

    g_hi[:, at], g_lo[:, at] = split(grads(t_hi, t_lo, q_h, q_l))
    g_hi[:, at_v], g_lo[:, at_v] = split(grads(w_hi, w_lo, d_h, d_l))
    flip = lambda x: x.astype(F32).T.astype(BF16)
    vt_h, vt_l = flip(v_h), flip(v_l)
    out = nn_dot(jnp.concatenate([vt_h, vt_l], axis=0), w_hi[...])
    out = out[:128] + out[128:] + nn_dot(vt_h, w_lo[...])
    att_ref[:, at] = jnp.concatenate([out[:64, :count], out[64:, count:]], axis=0).T


def main_kernel(mask_ref, own_ref, far_ref, q_ref, d_ref, w_ref, att_ref, grad_ref,
                a_hi, a_lo, at_hi, at_lo, kv_hi, kv_lo, g_hi, g_lo, s_ref, c_ref, w_hi, w_lo, t_hi, t_lo,
                term, core_in, total, ax_in, ax_sum, ay_in, by_in, by_sum, bx_in, z_out, z_in,
                core_s, core_r, ax_s, ax_r, ay_s, ay_r, by_s, by_r, bx_s, bx_r, z_s, z_r):
    ctx, doc = lax.axis_index("ctx"), lax.axis_index("doc")
    z, yhi, core = ctx // 4, (ctx // 2) % 2, ctx % 2
    x, ylo = doc // 2, doc % 2
    y = yhi * 2 + ylo

    def device(x_, y_, z_, core_):
        return {"ctx": z_ * 4 + (y_ // 2) * 2 + core_, "doc": x_ * 2 + y_ % 2}

    core_dev = device(x, y, z, 1 - core)
    x_dev = [None] + [device((x + n) % 4, y, z, core) for n in range(1, 4)]
    y_dev = [None] + [device(x, (y + n) % 4, z, core) for n in range(1, 4)]
    z_dev = [None] + [device(x, y, (z + n) % 8, core) for n in range(1, 8)]
    barrier = pltpu.get_barrier_semaphore()
    peers = [core_dev] + x_dev[1:] + y_dev[1:] + z_dev[1:]
    for peer in peers:
        pl.semaphore_signal(barrier, inc=1, device_id=peer, device_id_type=MESH)

    count = own_ref.shape[0]
    for n, ref in enumerate((own_ref, far_ref)):
        rows = pl.ds(n * count, count)
        a_hi[rows, :], a_lo[rows, :] = split(ref[...])
        at_hi[:, rows], at_lo[:, rows] = split(ref[...].T)

    def project(n, carry):
        at = pl.ds(pl.multiple_of(n * 256, 256), 256)
        p_h, p_l = split(w_ref[:, at])
        pairs = nn_dot(a_hi[...], p_h) + nn_dot(a_hi[...], p_l) + nn_dot(a_lo[...], p_h)
        kv_hi[:, at], kv_lo[:, at] = split(pairs)
        return carry

    lax.fori_loop(0, 4, project, 0)
    pl.semaphore_wait(barrier, len(peers))

    def pair_step(pair, carry):
        attend(mask_ref, kv_hi, kv_lo, q_ref, d_ref, att_ref, g_hi, g_lo, s_ref, c_ref, w_hi, w_lo, t_hi, t_lo, pair)
        return carry

    core_cp, ax_cp, ay_cp, by_cp, bx_cp, z_cp = {}, {}, {}, {}, {}, {}

    def term_step(block):
        at = pl.ds(block * 256, 256)
        value = nn_dot(at_hi[...], g_hi[:, at]) + nn_dot(at_hi[...], g_lo[:, at]) + nn_dot(at_lo[...], g_hi[:, at])
        value = value.reshape(8, 2, 2, 2, 16, 256)
        for c in range(2):
            for part in range(2):
                for yh in range(2):
                    for yl in range(2):
                        term[block, c, part, yh * 2 + yl] = value[:, yh, c, part, :, yl * 128:(yl + 1) * 128]
        core_cp[block] = remote(term.at[block, 1 - core], core_in.at[block], core_s.at[block], core_r.at[block], core_dev)
        core_cp[block].start()

    def sum_step(block):
        core_cp[block].wait_recv()
        total[block] = term[block, core] + core_in[block]

        @pl.when(block != x)
        def _():
            n = (block - x + 4) % 4
            remote(total.at[block, 0], ax_in.at[n - 1], ax_s.at[n - 1], ax_r.at[n - 1],
                   device(block, y, z, core)).start()

        for n in range(1, 4):
            by_cp[block, n] = remote(total.at[block, 1, (y + n) % 4], by_in.at[n - 1, block],
                                     by_s.at[n - 1, block], by_r.at[n - 1, block], y_dev[n])
            by_cp[block, n].start()

    lax.fori_loop(0, 2, pair_step, 0)
    term_step(0)
    term_step(2)
    lax.fori_loop(2, 4, pair_step, 0)
    sum_step(0)
    sum_step(2)
    term_step(1)
    term_step(3)
    sum_step(1)
    sum_step(3)

    value = total[x, 0]
    for n in range(1, 4):
        ax_cp[n] = remote(total.at[0, 0], ax_in.at[n - 1], ax_s.at[n - 1], ax_r.at[n - 1], x_dev[n])
        ax_cp[n].wait_recv()
        value = value + ax_in[n - 1]
    ax_sum[...] = value
    for n in range(1, 4):
        ay_cp[n] = remote(ax_sum.at[(y + n) % 4], ay_in.at[n - 1], ay_s.at[n - 1], ay_r.at[n - 1], y_dev[n])
        ay_cp[n].start()
    for block in range(4):
        value = total[block, 1, y]
        for n in range(1, 4):
            by_cp[block, n].wait_recv()
            value = value + by_in[n - 1, block]
        by_sum[block] = value
    for n in range(1, 4):
        bx_cp[n] = remote(by_sum.at[(x + n) % 4], bx_in.at[n - 1], bx_s.at[n - 1], bx_r.at[n - 1], x_dev[n])
        bx_cp[n].start()
    value = ax_sum[y]
    for n in range(1, 4):
        ay_cp[n].wait_recv()
        value = value + ay_in[n - 1]
    z_out[:, 0] = value
    value = by_sum[x]
    for n in range(1, 4):
        bx_cp[n].wait_recv()
        value = value + bx_in[n - 1]
    z_out[:, 1] = value
    for n in range(1, 8):
        z_cp[n] = remote(z_out.at[(z + n) % 8], z_in.at[n - 1], z_s.at[n - 1], z_r.at[n - 1], z_dev[n])
        z_cp[n].start()
    value = z_out[z]
    for n in range(1, 8):
        z_cp[n].wait_recv()
        value = value + z_in[n - 1]
    grad_ref[...] = value.reshape(32, 128) * (1.0 / 256.0)
    for copies in (core_cp, ax_cp, ay_cp, by_cp, bx_cp, z_cp):
        for copy in copies.values():
            copy.wait_send()


def attend_and_reduce(own, far, queries, cotangent, w_kv, mask):
    count, depth = own.shape
    vmem = pl.BlockSpec(memory_space=pltpu.VMEM)
    dma = pltpu.SemaphoreType.DMA
    f32 = lambda *shape: pltpu.VMEM(shape, F32)
    b16 = lambda *shape: pltpu.VMEM(shape, BF16)
    return pl.pallas_call(
        main_kernel,
        out_shape=(jax.ShapeDtypeStruct(queries.shape, F32), jax.ShapeDtypeStruct((32, 128), F32)),
        in_specs=[pl.BlockSpec(memory_space=pltpu.SMEM)] + [vmem] * 5,
        out_specs=(vmem, vmem),
        scratch_shapes=[
            b16(512, 1024), b16(512, 1024), b16(1024, 512), b16(1024, 512),
            b16(512, 1024), b16(512, 1024), b16(512, 1024), b16(512, 1024),
            f32(512, 512), f32(512, 512), b16(512, 512), b16(512, 512), b16(512, 512), b16(512, 512),
            f32(4, 2, 2, 4, 8, 16, 128), f32(4, 2, 4, 8, 16, 128), f32(4, 2, 4, 8, 16, 128),
            f32(3, 4, 8, 16, 128), f32(4, 8, 16, 128), f32(3, 8, 16, 128),
            f32(3, 4, 8, 16, 128), f32(4, 8, 16, 128), f32(3, 8, 16, 128),
            f32(8, 2, 16, 128), f32(7, 2, 16, 128),
            dma((4,)), dma((4,)), dma((3,)), dma((3,)), dma((3,)), dma((3,)),
            dma((3, 4)), dma((3, 4)), dma((3,)), dma((3,)), dma((7,)), dma((7,)),
        ],
        compiler_params=pltpu.CompilerParams(collective_id=1, has_side_effects=True, vmem_limit_bytes=56 * MIB),
    )(mask, own, far, queries, cotangent, w_kv)


def shards(activations, queries, d_out, w_kv, partner, block_mask):
    act = activations[0]
    far = exchange(act, partner)
    attended, gradient = attend_and_reduce(act, far, queries[0], d_out[0], w_kv, block_mask[0, 0])
    return attended[None], gradient


def solution(mesh):
    return jax.shard_map(
        shards,
        mesh=mesh,
        in_specs=(
            P("doc", "ctx", None), P("doc", "ctx", None), P("doc", "ctx", None),
            P(), P("doc", "ctx"), P("doc", "ctx", None, None),
        ),
        out_specs=(P("doc", "ctx", None), P("ctx", "doc")),
        check_vma=False,
    )
```

time: 546 us -> 126 us (0.23)
  waiting for transfers between devices: 440 us -> 0 us
  Pallas kernels: 0 us -> 118 us
  matrix products: 36.1 us -> 0 us
  starting transfers between devices: 23.8 us -> 0 us
  local copies, waits for them, and re-layouts: 20.2 us -> 5.38 us
  between operations: 14.9 us -> 1.31 us
  other arithmetic: 8.42 us -> 0 us
    ppermute x10 -> x0, waiting for transfers between devices: 277 us -> none  [from_partner(): return lax.ppermute(value, axis, pairs)]
    unnamed x3 -> x0, waiting for transfers between devices: 127 us -> none
    pallas_call x0 -> x2, Pallas kernels: none -> 118 us  [the longest x1 65.5 us: exchange(): pl.pallas_call(exchange_kernel, out_shape=jax.ShapeDtypeStruct((count, de...]
    dot_general x7 -> x0, matrix products: 36.1 us -> none  [the longest x1 6.08 us: attend_shard(): jnp.einsum('hqk,qhd->khd', weights, cotangent, precision=highest)]
    reduce_scatter x1 -> x0, waiting for transfers between devices: 35.7 us -> none  [shards(): lax.psum_scatter(partial_sum, 'doc', scatter_dimension=1, tiled=True)]
    ppermute x10 -> x0, starting transfers between devices: 23.8 us -> none  [from_partner(): return lax.ppermute(value, axis, pairs)]
    unnamed x22 -> x6, local copies, waits for them, and re-layouts: 15.1 us -> 5.38 us
    select_n x9 -> x0, other arithmetic: 6.29 us -> none  [the longest x5 5.62 us: shards(): jnp.where(jnp.right_shift(offset, bit_index) % 2 == 1, moved, far_pairs)]
  transfers between devices with their start and end apart: 12 -> 0, of which waited for: 12 -> 0; matrix products, arithmetic and copies ran while one was open for 1% -> 0% of each run, Pallas kernels for 0% -> 0%
where the time goes in v1:
time: 126 us; the launch traced here: 125 us
  Pallas kernels  118 us (94%)
  local copies, waits for them, and re-layouts  5.38 us (4%)
  between operations  1.31 us (1%)
    pallas_call x1, Pallas kernels, exchange(): pl.pallas_call(exchange_kernel, out_shape=jax.ShapeDtypeStruct((count, de...  65.5 us
    pallas_call x1, Pallas kernels, attend_and_reduce(): pl.pallas_call(main_kernel, out_shape=(jax.ShapeDtypeStruct(queries.shape...  52.8 us
    unnamed x6, local copies, waits for them, and re-layouts  5.38 us

profile of v1, /device:TPU:2, one launch (start us, length us, event | category | flops | bytes accessed | tf_op | source)
XLA Modules:
  0.0 125.0 jit_solution(14015178462472827762)
XLA Ops:
  1.3 0.0 copy-start
  1.3 1.2 copy-done
  2.5 65.5 %shard_map.77.far_ref = f32[256,1024]{1,0:T(8,128)S(1)} custom-call(s32[1,1]{1,0:T(1,128)S(6)} %copy.10.partner_ref, f32[256,1024]{1,0:T(8,128)S(1)} %bitcast.6), custom_call_target="tpu_custom_call" | custom-call | tf_op jit(solution)/shard_map/pallas_call | solution.py:164
  68.0 0.0 copy-start.1
  68.0 1.0 copy-done.1
  68.9 52.8 %shard_map.78 = (f32[256,512]{1,0:T(8,128)}, f32[32,128]{1,0:T(8,128)}) custom-call(s32[4,4]{1,0:T(4,128)} %bitcast.10, f32[256,1024]{1,0:T(8,128)} %bitcast.5, f32[256,1024]{1,0:T(8,128)} %copy-done.1, f32[256,512]{1,0:T(8,128)} %bitcast.8, f32[256,512]{1,0:T(8,128)} %bitcast.9, f32[1024,1024]{1,0:T(8,128)} %w_ref.1), custom_call_target="tpu_custom_call" | custom-call | tf_op jit(solution)/shard_map/pallas_call | solution.py:364
  121.8 1.9 %copy.11 = f32[1,256,512]{2,1,0:T(8,128)} copy(f32[1,256,512]{2,1,0:T(8,128)} %bitcast.7) | data formatting | bytes 1048576
  123.7 1.3 %copy.12 = f32[32,128]{1,0:T(8,128)} copy(f32[32,128]{1,0:T(8,128)} %get-tuple-element.9) | data formatting | bytes 32768
Async XLA Ops:
  1.3 1.2 copy-start
  68.0 1.0 copy-start.1

commit v2 on v0

v2 whole, which is shorter than its diff:
```python
import functools

import jax
import jax.numpy as jnp
from jax import lax
from jax.experimental import pallas as pl
from jax.experimental.pallas import tpu as pltpu
from jax.sharding import PartitionSpec as P

MESH = pl.DeviceIdType.MESH
F32, BF16 = jnp.float32, jnp.bfloat16
MASKED = -1e30
SLOTS = 16
CHUNKS = 8
MIB = 1024 * 1024


def split(x):
    hi = x.astype(BF16)
    return hi, (x - hi.astype(F32)).astype(BF16)


def nt_dot(a, b):
    return lax.dot_general(a, b, (((1,), (1,)), ((), ())), preferred_element_type=F32)


def nn_dot(a, b):
    return lax.dot_general(a, b, (((1,), (0,)), ((), ())), preferred_element_type=F32)


def remote(src, dst, send_sem, recv_sem, device):
    return pltpu.make_async_remote_copy(
        src_ref=src, dst_ref=dst, send_sem=send_sem, recv_sem=recv_sem,
        device_id=device, device_id_type=MESH,
    )


def head_pair(x, first):
    return split(jnp.concatenate([jnp.where(first, x, 0.0), jnp.where(first, 0.0, x)], axis=0))


def cat(*parts):
    return jnp.concatenate(parts, axis=1)


def scores(kv_hi, kv_lo, rows, at, right_h, right_l):
    hi, lo = kv_hi[rows, at], kv_lo[rows, at]
    return nt_dot(cat(hi, hi, lo), cat(right_h, right_l, right_h))


def lanes_of(pair, start=0):
    return pl.ds(pl.multiple_of(start + pair * 128, 128), 128)


BLOCK = 64


def own_part(pair, kv_hi, kv_lo, q_ref, d_ref, s_own, c_own, stats):
    count, half = q_ref.shape[0], kv_hi.shape[1] // 2
    first = lax.broadcasted_iota(jnp.int32, (count, 128), 1) < 64
    at, at_v = lanes_of(pair), lanes_of(pair, half)
    q_h, q_l = head_pair(q_ref[:, at] * 0.125, first)
    d_h, d_l = head_pair(d_ref[:, at], first)
    own = pl.ds(0, count)
    s_own[pair] = scores(kv_hi, kv_lo, own, at, q_h, q_l)
    c_own[pair] = scores(kv_hi, kv_lo, own, at_v, d_h, d_l)
    maximum = jnp.max(s_own[pair, pl.ds(0, BLOCK), :], axis=0, keepdims=True)
    for b in range(1, count // BLOCK):
        maximum = jnp.maximum(maximum, jnp.max(s_own[pair, pl.ds(b * BLOCK, BLOCK), :], axis=0, keepdims=True))
    total, dots = 0.0, 0.0
    for b in range(count // BLOCK):
        rows = pl.ds(b * BLOCK, BLOCK)
        raised = jnp.exp(s_own[pair, rows, :] - maximum)
        s_own[pair, rows, :] = raised
        total = total + jnp.sum(raised, axis=0, keepdims=True)
        dots = dots + jnp.sum(raised * c_own[pair, rows, :], axis=0, keepdims=True)
    stats[pair, pl.ds(0, 1), :] = maximum
    stats[pair, pl.ds(1, 1), :] = total
    stats[pair, pl.ds(2, 1), :] = dots


def far_part(pair, mask_ref, kv_hi, kv_lo, q_ref, d_ref, s_own, c_own, stats, s_far, c_far,
             w_hi, w_lo, t_hi, t_lo, att, g_hi, g_lo):
    count, half = q_ref.shape[0], kv_hi.shape[1] // 2
    first = lax.broadcasted_iota(jnp.int32, (count, 128), 1) < 64
    at, at_v = lanes_of(pair), lanes_of(pair, half)
    q_h, q_l = head_pair(q_ref[:, at] * 0.125, first)
    d_h, d_l = head_pair(d_ref[:, at], first)
    far = pl.ds(count, count)
    s_far[...] = scores(kv_hi, kv_lo, far, at, q_h, q_l)
    c_far[...] = scores(kv_hi, kv_lo, far, at_v, d_h, d_l)
    lanes = lax.broadcasted_iota(jnp.int32, (1, 2 * count), 1) % count // BLOCK
    own_max = stats[pair, pl.ds(0, 1), :]
    maximum = own_max
    blocks = count // BLOCK
    for b in range(blocks):
        rows = pl.ds(b * BLOCK, BLOCK)
        seen = jnp.where(lanes == 0, mask_ref[0, b], jnp.where(lanes == 1, mask_ref[1, b], jnp.where(
            lanes == 2, mask_ref[2, b], mask_ref[3, b])))
        piece = jnp.where(seen == 1, s_far[rows, :], MASKED)
        s_far[rows, :] = piece
        maximum = jnp.maximum(maximum, jnp.max(piece, axis=0, keepdims=True))
    shrink = jnp.exp(own_max - maximum)
    total = stats[pair, pl.ds(1, 1), :] * shrink
    dots = stats[pair, pl.ds(2, 1), :] * shrink
    for b in range(blocks):
        rows = pl.ds(b * BLOCK, BLOCK)
        raised = jnp.exp(s_far[rows, :] - maximum)
        s_far[rows, :] = raised
        total = total + jnp.sum(raised, axis=0, keepdims=True)
        dots = dots + jnp.sum(raised * c_far[rows, :], axis=0, keepdims=True)
    inverse = 1.0 / total
    row_dot = dots * inverse
    own_scale = shrink * inverse
    for b in range(blocks):
        rows = pl.ds(b * BLOCK, BLOCK)
        weight = s_own[pair, rows, :] * own_scale
        w_hi[rows, :], w_lo[rows, :] = split(weight)
        t_hi[rows, :], t_lo[rows, :] = split(weight * (c_own[pair, rows, :] - row_dot))
        lower = pl.ds(count + b * BLOCK, BLOCK)
        weight = s_far[rows, :] * inverse
        w_hi[lower, :], w_lo[lower, :] = split(weight)
        t_hi[lower, :], t_lo[lower, :] = split(weight * (c_far[rows, :] - row_dot))

    def grads(left_hi, left_lo, right_h, right_l):
        both = nn_dot(left_hi[...], cat(right_h, right_l))
        return both[:, :128] + both[:, 128:] + nn_dot(left_lo[...], right_h)

    g_hi[:, :128], g_lo[:, :128] = split(grads(t_hi, t_lo, q_h, q_l))
    g_hi[:, 128:], g_lo[:, 128:] = split(grads(w_hi, w_lo, d_h, d_l))
    flip = lambda value: value.astype(F32).T.astype(BF16)
    vt_h, vt_l = flip(kv_hi[:, at_v]), flip(kv_lo[:, at_v])
    out = nn_dot(jnp.concatenate([vt_h, vt_l], axis=0), w_hi[...])
    out = out[:128] + out[128:] + nn_dot(vt_h, w_lo[...])
    att[:, at] = jnp.concatenate([out[:64, :count], out[64:, count:]], axis=0).T


def kernel(partner_ref, mask_ref, act_hbm, q_hbm, d_hbm, w_hbm, att_hbm, grad_ref,
           act, far, q_ref, d_ref, w_ref, core_in, base, y_in, z_out, z_in, dest,
           p_hi, p_lo, a_hi, a_lo, at_hi, at_lo, kv_hi, kv_lo, g_hi, g_lo, s_own, c_own, stats, s_far, c_far,
           w_hi, w_lo, t_hi, t_lo, att,
           term, half_in, total, ax_in, ax_sum, ay_in, by_in, by_sum, bx_in, r_out, r_in,
           load_s, core_s, core_r, y_s, y_r, z_s, z_r,
           half_s, half_r, ax_s, ax_r, ay_s, ay_r, by_s, by_r, bx_s, bx_r, r_s, r_r):
    ctx, doc = lax.axis_index("ctx"), lax.axis_index("doc")
    z, yhi, core = ctx // 4, (ctx // 2) % 2, ctx % 2
    x, ylo = doc // 2, doc % 2
    y = yhi * 2 + ylo

    def device(x_, y_, z_, core_):
        return {"ctx": z_ * 4 + (y_ // 2) * 2 + core_, "doc": x_ * 2 + y_ % 2}

    core_dev = device(x, y, z, 1 - core)
    x_dev = [None] + [device((x + n) % 4, y, z, core) for n in range(1, 4)]
    y_dev = [None] + [device(x, (y + n) % 4, z, core) for n in range(1, 4)]
    z_dev = [None] + [device(x, y, (z + n) % 8, core) for n in range(1, 8)]
    far_y = y_dev[2]
    ring_dev = (z_dev[1], z_dev[7])
    barrier = pltpu.get_barrier_semaphore()
    peers = [core_dev] + x_dev[1:] + y_dev[1:] + z_dev[1:]
    for peer in peers:
        pl.semaphore_signal(barrier, inc=1, device_id=peer, device_id_type=MESH)
    loads = [pltpu.make_async_copy(src, dst, load_s.at[n]) for n, (src, dst) in enumerate(
        ((act_hbm, act), (w_hbm, w_ref), (q_hbm, q_ref), (d_hbm, d_ref)))]
    for load in loads:
        load.start()

    offset = jnp.bitwise_xor(partner_ref[0, 0], ctx)
    flip_core = offset % 2 == 1
    flip_y = (offset // 2) % 2 == 1
    sz = offset // 4
    both_ = jnp.logical_and
    either = jnp.logical_or
    is4, is5 = sz == 4, sz == 5
    two = either(sz == 2, sz == 6)
    three = either(sz == 3, sz == 7)
    steady = either(either(is4, is5), three)
    facing = (z, 7 - z)
    role = [jnp.where(sz >= 6, (zd + 2) % 4, zd % 4) for zd in facing]
    odd = [zd % 2 == 1 for zd in facing]
    count = act.shape[0]
    rows = count // CHUNKS
    core_cp, y_cp, z_cp, done = {}, {}, {}, set()

    def once(key, copy):
        if key not in done:
            done.add(key)
            copy.wait_recv()

    def chunk(ref, j):
        return ref[pl.ds(j * rows, rows), :]

    def send_core(j, src):
        core_cp[j] = remote(src, core_in.at[j], core_s.at[j], core_r.at[j], core_dev)
        core_cp[j].start()

    def send_y(j, src):
        y_cp[j] = remote(src, y_in.at[j], y_s.at[j], y_r.at[j], far_y)
        y_cp[j].start()

    def swap_core(j, value):
        once(("core", j), core_cp[j])
        return jnp.where(flip_core, core_in[j], value)

    def swap_y(j, value):
        once(("y", j), y_cp[j])
        return jnp.where(flip_y, y_in[j], value)

    def own(j):
        if j < 2:
            return chunk(act, j)
        return base[j] if j < 4 else swap_y(j, base[j])

    def got(t):
        for d in range(2):
            once((d, t), z_cp[d, t])

    def slot(t):
        for d in range(2):
            if t < 4:
                value = own(t) if d == t == 0 else jnp.where(is4, own(2 * t + d), own(t))
            elif t < 8:
                relay = either(is4, either(both_(is5, jnp.logical_not(odd[d])), both_(three, role[d] == 1)))
                value = jnp.where(relay, z_in[d, t - 4], own(t))
            else:
                value = jnp.where(steady, z_in[d, t - 4], z_in[d, t - 8])
                if t >= 12:
                    value = jnp.where(both_(three, role[d] == 1), own(t - 8), value)
            z_out[d, t] = value
            z_cp[d, t] = remote(z_out.at[d, t], z_in.at[d, t], z_s.at[d, t], z_r.at[d, t], ring_dev[d])
            z_cp[d, t].start()

    def arrived(k):
        value = own(k)
        for d in range(2):
            early = both_(sz == 1, odd[d])
            late = either(both_(two, role[d] >= 2),
                          either(both_(three, role[d] == 3), both_(is5, jnp.logical_not(odd[d]))))
            near = both_(three, role[d] == 2)
            if k < 4:
                early = either(early, near)
            else:
                late = either(late, near)
            value = jnp.where(early, z_in[d, k], value)
            value = jnp.where(late, z_in[d, 8 + k], value)
        return jnp.where(is4, z_in[k % 2, 12 + k // 2], value)

    def set_far(k, value):
        far[pl.ds(k * rows, rows), :] = value

    half = count // 2

    def take(ref, start, into, size):
        a_hi[pl.ds(into, size), :], a_lo[pl.ds(into, size), :] = split(ref[pl.ds(start, size), :])
        at_hi[:, pl.ds(into, size)], at_lo[:, pl.ds(into, size)] = split(ref[pl.ds(start, size), :].T)

    def project(start, size, fresh):
        def step(n, carry):
            at = pl.ds(pl.multiple_of(n * 256, 256), 256)
            if fresh:
                p_hi[:, at], p_lo[:, at] = split(w_ref[:, at])
            rows_ = pl.ds(start, size)
            hi, lo = a_hi[rows_, :], a_lo[rows_, :]
            pairs = nn_dot(hi, p_hi[:, at]) + nn_dot(hi, p_lo[:, at]) + nn_dot(lo, p_hi[:, at])
            kv_hi[rows_, at], kv_lo[rows_, at] = split(pairs)
            return carry
        lax.fori_loop(0, 4, step, 0)

    def own_pairs(start, stop):
        def step(pair, carry):
            own_part(pair, kv_hi, kv_lo, q_ref, d_ref, s_own, c_own, stats)
            return carry
        lax.fori_loop(start, stop, step, 0)

    loads[0].wait()
    pl.semaphore_wait(barrier, len(peers))
    for j in (4, 5, 2, 3, 6, 7):
        send_core(j, act.at[pl.ds(j * rows, rows)])
    slot(0)
    for j in (4, 5, 2, 3, 6, 7):
        base[j] = swap_core(j, chunk(act, j))
        if j >= 4:
            send_y(j, base.at[j])
        elif j == 3:
            slot(1)
    slot(2)
    slot(3)
    take(act, 0, 0, count)
    loads[1].wait()
    got(0)
    slot(4)
    project(0, count, True)
    loads[2].wait()
    loads[3].wait()
    got(1)
    slot(5)
    own_pairs(0, 2)
    got(2)
    slot(6)
    own_pairs(2, 4)
    for t in range(7, SLOTS):
        got(t - 4)
        slot(t)
    got(12)
    for k in range(2):
        dest[k] = arrived(k)
        send_y(k, dest.at[k])
    got(13)
    for k in range(2, 4):
        dest[k] = arrived(k)
        send_y(k, dest.at[k])
    for k in range(2):
        base[k] = swap_y(k, dest[k])
        send_core(k, base.at[k])
    for k in range(2, 4):
        set_far(k, swap_y(k, dest[k]))
    for k in range(2):
        set_far(k, swap_core(k, base[k]))
    take(far, 0, count, half)
    project(count, half, False)
    got(14)
    for k in range(4, 6):
        set_far(k, arrived(k))
    got(15)
    for k in range(6, 8):
        set_far(k, arrived(k))
    take(far, half, count + half, half)
    project(count + half, half, False)

    last = 2 * (x % 2) + ylo
    half_cp, ax_cp, ay_cp, by_cp, bx_cp, r_cp = {}, {}, {}, {}, {}, {}

    def pair_of(i):
        return (last + 1 + i) % 4

    def pair_step(i):
        far_part(pair_of(i), mask_ref, kv_hi, kv_lo, q_ref, d_ref, s_own, c_own, stats, s_far, c_far,
                 w_hi, w_lo, t_hi, t_lo, att, g_hi, g_lo)
        value = nn_dot(at_hi[...], g_hi[...]) + nn_dot(at_hi[...], g_lo[...]) + nn_dot(at_lo[...], g_hi[...])
        value = value.reshape(8, 2, 2, 2, 16, 256)
        for c in range(2):
            for kind in range(2):
                for part in range(2):
                    for yh in range(2):
                        term[i, c, kind, part, yh] = value[:, yh, c, part, :, kind * 128:(kind + 1) * 128]

    def half_copy(i):
        return remote(term.at[i, 1 - core], half_in.at[i], half_s.at[i], half_r.at[i], core_dev)

    def moves(i):
        pair = pair_of(i)
        found = []
        for kind in range(2):
            to_x = 2 * kind + pair // 2
            n = (to_x - x + 4) % 4
            slot_n = (n + 3) % 4 % 3
            found.append((n != 0, remote(total.at[i, kind, 0], ax_in.at[slot_n, pair % 2], ax_s.at[i, kind],
                                         ax_r.at[slot_n, pair % 2], device(to_x, y, z, core))))
            for yh in range(2):
                to_y = yh * 2 + pair % 2
                m = (to_y - y + 4) % 4
                slot_m = (m + 3) % 4 % 3
                found.append((m != 0, remote(total.at[i, kind, 1, yh], by_in.at[slot_m, to_x], by_s.at[i, kind, yh],
                                             by_r.at[slot_m, to_x], device(x, to_y, z, core))))
        return found

    def sum_step(i):
        half_copy(i).wait_recv()
        total[i] = term[i, core] + half_in[i]
        for condition, copy in moves(i):
            pl.when(condition)(copy.start)

    for i in range(4):
        pair_step(i)
        half_copy(i).start()
        if i > 0:
            sum_step(i - 1)
    out_copy = pltpu.make_async_copy(att, att_hbm, load_s.at[4])
    out_copy.start()
    sum_step(3)

    mine = x // 2
    for yl in range(2):
        i = (2 * (x % 2) + yl - last + 3) % 4
        value = total[i, mine, 0]
        for n in range(1, 4):
            remote(total.at[0, 0, 0], ax_in.at[n - 1, yl], ax_s.at[0, 0], ax_r.at[n - 1, yl], x_dev[n]).wait_recv()
            value = value + ax_in[n - 1, yl]
        for yh in range(2):
            ax_sum[yh * 2 + yl] = value[yh]
    for n in range(1, 4):
        ay_cp[n] = remote(ax_sum.at[(y + n) % 4], ay_in.at[n - 1], ay_s.at[n - 1], ay_r.at[n - 1], y_dev[n])
        ay_cp[n].start()
    for to_x in range(4):
        i = (2 * (to_x % 2) + ylo - last + 3) % 4
        value = total[i, to_x // 2, 1, yhi]
        for n in range(1, 4):
            remote(total.at[0, 0, 1, 0], by_in.at[n - 1, to_x], by_s.at[0, 0, 0], by_r.at[n - 1, to_x],
                   y_dev[n]).wait_recv()
            value = value + by_in[n - 1, to_x]
        by_sum[to_x] = value
    for n in range(1, 4):
        bx_cp[n] = remote(by_sum.at[(x + n) % 4], bx_in.at[n - 1], bx_s.at[n - 1], bx_r.at[n - 1], x_dev[n])
        bx_cp[n].start()
    value = ax_sum[y]
    for n in range(1, 4):
        ay_cp[n].wait_recv()
        value = value + ay_in[n - 1]
    r_out[:, 0] = value
    value = by_sum[x]
    for n in range(1, 4):
        bx_cp[n].wait_recv()
        value = value + bx_in[n - 1]
    r_out[:, 1] = value
    for n in range(1, 8):
        r_cp[n] = remote(r_out.at[(z + n) % 8], r_in.at[n - 1], r_s.at[n - 1], r_r.at[n - 1], z_dev[n])
        r_cp[n].start()
    for copies in (core_cp, y_cp, z_cp, ay_cp, bx_cp):
        for copy in copies.values():
            copy.wait_send()
    for i in range(4):
        half_copy(i).wait_send()
        for condition, copy in moves(i):
            pl.when(condition)(copy.wait_send)
    out_copy.wait()
    value = r_out[z]
    for n in range(1, 8):
        r_cp[n].wait_recv()
        value = value + r_in[n - 1]
    grad_ref[...] = value.reshape(32, 128) * (1.0 / 256.0)
    for copy in r_cp.values():
        copy.wait_send()


def run(act, queries, cotangent, w_kv, partner, mask):
    count, depth = act.shape
    width = queries.shape[1]
    rows = count // CHUNKS
    anywhere = pl.BlockSpec(memory_space=pl.ANY)
    smem = pl.BlockSpec(memory_space=pltpu.SMEM)
    vmem = pl.BlockSpec(memory_space=pltpu.VMEM)
    dma = lambda *shape: pltpu.SemaphoreType.DMA(shape)
    f32 = lambda *shape: pltpu.VMEM(shape, F32)
    b16 = lambda *shape: pltpu.VMEM(shape, BF16)
    keys, pairs = 2 * count, width // 128
    return pl.pallas_call(
        kernel,
        out_shape=(jax.ShapeDtypeStruct((count, width), F32), jax.ShapeDtypeStruct((32, 128), F32)),
        in_specs=[smem, smem] + [anywhere] * 4,
        out_specs=(anywhere, vmem),
        scratch_shapes=[
            f32(count, depth), f32(count, depth), f32(count, width), f32(count, width), f32(depth, 2 * width),
            f32(CHUNKS, rows, depth), f32(CHUNKS, rows, depth), f32(CHUNKS, rows, depth),
            f32(2, SLOTS, rows, depth), f32(2, SLOTS, rows, depth), f32(4, rows, depth),
            b16(depth, 2 * width), b16(depth, 2 * width), b16(keys, depth), b16(keys, depth),
            b16(depth, keys), b16(depth, keys), b16(keys, 2 * width), b16(keys, 2 * width),
            b16(keys, 256), b16(keys, 256), f32(pairs, count, keys), f32(pairs, count, keys), f32(pairs, 8, keys),
            f32(count, keys), f32(count, keys), b16(keys, keys), b16(keys, keys), b16(keys, keys), b16(keys, keys),
            f32(count, width),
            f32(4, 2, 2, 2, 2, 8, 16, 128), f32(4, 2, 2, 2, 8, 16, 128), f32(4, 2, 2, 2, 8, 16, 128),
            f32(3, 2, 2, 8, 16, 128), f32(4, 8, 16, 128), f32(3, 8, 16, 128),
            f32(3, 4, 8, 16, 128), f32(4, 8, 16, 128), f32(3, 8, 16, 128),
            f32(8, 2, 16, 128), f32(7, 2, 16, 128),
            dma(5), dma(CHUNKS), dma(CHUNKS), dma(CHUNKS), dma(CHUNKS), dma(2, SLOTS), dma(2, SLOTS),
            dma(4), dma(4), dma(4, 2), dma(3, 2), dma(3), dma(3), dma(4, 2, 2), dma(3, 4), dma(3), dma(3), dma(7), dma(7),
        ],
        compiler_params=pltpu.CompilerParams(collective_id=0, has_side_effects=True, vmem_limit_bytes=60 * MIB),
    )(partner, mask, act, queries, cotangent, w_kv)


def shards(activations, queries, d_out, w_kv, partner, block_mask):
    attended, gradient = run(activations[0], queries[0], d_out[0], w_kv, partner, block_mask[0, 0])
    return attended[None], gradient


def solution(mesh):
    return jax.shard_map(
        shards,
        mesh=mesh,
        in_specs=(
            P("doc", "ctx", None), P("doc", "ctx", None), P("doc", "ctx", None),
            P(), P("doc", "ctx"), P("doc", "ctx", None, None),
        ),
        out_specs=(P("doc", "ctx", None), P("ctx", "doc")),
        check_vma=False,
    )
```

time: 546 us -> 112 us (0.21)
  waiting for transfers between devices: 440 us -> 0 us
  Pallas kernels: 0 us -> 107 us
  matrix products: 36.1 us -> 0 us
  starting transfers between devices: 23.8 us -> 0 us
  local copies, waits for them, and re-layouts: 20.2 us -> 3.19 us
  between operations: 14.9 us -> 1.29 us
  other arithmetic: 8.42 us -> 0 us
    ppermute x10 -> x0, waiting for transfers between devices: 277 us -> none  [from_partner(): return lax.ppermute(value, axis, pairs)]
    unnamed x3 -> x0, waiting for transfers between devices: 127 us -> none
    pallas_call x0 -> x1, Pallas kernels: none -> 107 us  [run(): pl.pallas_call(kernel, out_shape=(jax.ShapeDtypeStruct((count, width), F3...]
    dot_general x7 -> x0, matrix products: 36.1 us -> none  [the longest x1 6.08 us: attend_shard(): jnp.einsum('hqk,qhd->khd', weights, cotangent, precision=highest)]
    reduce_scatter x1 -> x0, waiting for transfers between devices: 35.7 us -> none  [shards(): lax.psum_scatter(partial_sum, 'doc', scatter_dimension=1, tiled=True)]
    ppermute x10 -> x0, starting transfers between devices: 23.8 us -> none  [from_partner(): return lax.ppermute(value, axis, pairs)]
    unnamed x22 -> x2, local copies, waits for them, and re-layouts: 15.1 us -> 3.19 us
    select_n x9 -> x0, other arithmetic: 6.29 us -> none  [the longest x5 5.62 us: shards(): jnp.where(jnp.right_shift(offset, bit_index) % 2 == 1, moved, far_pairs)]
  transfers between devices with their start and end apart: 12 -> 0, of which waited for: 12 -> 0; matrix products, arithmetic and copies ran while one was open for 1% -> 0% of each run, Pallas kernels for 0% -> 0%
where the time goes in v2:
time: 112 us; the launch traced here: 111 us
  Pallas kernels  107 us (96%)
  local copies, waits for them, and re-layouts  3.19 us (3%)
  between operations  1.29 us (1%)
    pallas_call x1, Pallas kernels, run(): pl.pallas_call(kernel, out_shape=(jax.ShapeDtypeStruct((count, width), F3...  107 us
    unnamed x2, local copies, waits for them, and re-layouts  3.19 us

profile of v2, /device:TPU:2, one launch (start us, length us, event | category | flops | bytes accessed | tf_op | source)
XLA Modules:
  0.0 111.0 jit_solution(15379829988153143803)
XLA Ops:
  1.3 106.5 %shard_map.77 = (f32[256,512]{1,0:T(8,128)}, f32[32,128]{1,0:T(8,128)}) custom-call(s32[1,1]{1,0:T(1,128)S(6)} %copy.10.partner_ref, s32[4,4]{1,0:T(4,128)} %bitcast.9, f32[256,1024]{1,0:T(8,128)} %bitcast.5, f32[256,512]{1,0:T(8,128)} %bitcast.6, f32[256,512]{1,0:T(8,128)} %bitcast.7, f32[1024,1024]{1,0:T(8,128)} %w_hbm.1), custom_call_target="tpu_custom_call" | custom-call | tf_op jit(solution)/shard_map/pallas_call | solution.py:446
  107.8 1.9 %copy.11 = f32[1,256,512]{2,1,0:T(8,128)} copy(f32[1,256,512]{2,1,0:T(8,128)} %bitcast.8) | data formatting | bytes 1048576
  109.7 1.3 %copy.12 = f32[32,128]{1,0:T(8,128)} copy(f32[32,128]{1,0:T(8,128)} %get-tuple-element.9) | data formatting | bytes 32768

commit v3 on v2

--- a/solution.py
+++ b/solution.py
@@ -10,8 +10,8 @@
 MESH = pl.DeviceIdType.MESH
 F32, BF16 = jnp.float32, jnp.bfloat16
 MASKED = -1e30
-SLOTS = 16
-CHUNKS = 8
+SLOTS = 32
+CHUNKS = 16
 MIB = 1024 * 1024
 
 
@@ -174,7 +174,6 @@
     is4, is5 = sz == 4, sz == 5
     two = either(sz == 2, sz == 6)
     three = either(sz == 3, sz == 7)
-    steady = either(either(is4, is5), three)
     facing = (z, 7 - z)
     role = [jnp.where(sz >= 6, (zd + 2) % 4, zd % 4) for zd in facing]
     odd = [zd % 2 == 1 for zd in facing]
@@ -207,9 +206,7 @@
         return jnp.where(flip_y, y_in[j], value)
 
     def own(j):
-        if j < 2:
-            return chunk(act, j)
-        return base[j] if j < 4 else swap_y(j, base[j])
+        return chunk(act, j) if j < 8 else swap_y(j, base[j])
 
     def got(t):
         for d in range(2):
@@ -220,12 +217,15 @@
             if t < 4:
                 value = own(t) if d == t == 0 else jnp.where(is4, own(2 * t + d), own(t))
             elif t < 8:
-                relay = either(is4, either(both_(is5, jnp.logical_not(odd[d])), both_(three, role[d] == 1)))
-                value = jnp.where(relay, z_in[d, t - 4], own(t))
+                value = jnp.where(is4, z_in[d, t - 4], own(t))
+            elif t < 16:
+                relay = either(both_(is5, jnp.logical_not(odd[d])), both_(three, role[d] == 1))
+                value = jnp.where(is4, z_in[d, t - 4], jnp.where(relay, z_in[d, t - 8], own(t)))
             else:
-                value = jnp.where(steady, z_in[d, t - 4], z_in[d, t - 8])
-                if t >= 12:
-                    value = jnp.where(both_(three, role[d] == 1), own(t - 8), value)
+                value = jnp.where(either(is5, three), z_in[d, t - 8], z_in[d, t - 16])
+                if t >= 24:
+                    value = jnp.where(both_(three, role[d] == 1), own(t - 16), value)
+                value = jnp.where(is4, own(8 + 2 * (t - 16) + d) if t < 20 else z_in[d, t - 4], value)
             z_out[d, t] = value
             z_cp[d, t] = remote(z_out.at[d, t], z_in.at[d, t], z_s.at[d, t], z_r.at[d, t], ring_dev[d])
             z_cp[d, t].start()
@@ -237,13 +237,13 @@
             late = either(both_(two, role[d] >= 2),
                           either(both_(three, role[d] == 3), both_(is5, jnp.logical_not(odd[d]))))
             near = both_(three, role[d] == 2)
-            if k < 4:
+            if k < 8:
                 early = either(early, near)
             else:
                 late = either(late, near)
             value = jnp.where(early, z_in[d, k], value)
-            value = jnp.where(late, z_in[d, 8 + k], value)
-        return jnp.where(is4, z_in[k % 2, 12 + k // 2], value)
+            value = jnp.where(late, z_in[d, 16 + k], value)
+        return jnp.where(is4, z_in[k % 2, 12 + k // 2 if k < 8 else 24 + k // 2], value)
 
     def set_far(k, value):
         far[pl.ds(k * rows, rows), :] = value
@@ -252,9 +252,12 @@
 
     def take(ref, start, into, size):
         a_hi[pl.ds(into, size), :], a_lo[pl.ds(into, size), :] = split(ref[pl.ds(start, size), :])
-        at_hi[:, pl.ds(into, size)], at_lo[:, pl.ds(into, size)] = split(ref[pl.ds(start, size), :].T)
-
-    def project(start, size, fresh):
+        turned = ref[pl.ds(start, size), :].T.reshape(16, 2, 32, size)
+        for c in range(2):
+            hi, lo = split(turned[:, c].reshape(512, size))
+            at_hi[c, :, pl.ds(into, size)], at_lo[c, :, pl.ds(into, size)] = hi, lo
+
+    def project(start, size, fresh, n0, n1):
         def step(n, carry):
             at = pl.ds(pl.multiple_of(n * 256, 256), 256)
             if fresh:
@@ -264,68 +267,71 @@
             pairs = nn_dot(hi, p_hi[:, at]) + nn_dot(hi, p_lo[:, at]) + nn_dot(lo, p_hi[:, at])
             kv_hi[rows_, at], kv_lo[rows_, at] = split(pairs)
             return carry
-        lax.fori_loop(0, 4, step, 0)
-
-    def own_pairs(start, stop):
-        def step(pair, carry):
-            own_part(pair, kv_hi, kv_lo, q_ref, d_ref, s_own, c_own, stats)
+        lax.fori_loop(n0, n1, step, 0)
+
+    def own_pair(pair):
+        def step(n, carry):
+            own_part(n, kv_hi, kv_lo, q_ref, d_ref, s_own, c_own, stats)
             return carry
-        lax.fori_loop(start, stop, step, 0)
+        lax.fori_loop(pair, pair + 1, step, 0)
+
+    def work(t):
+        if t in (6, 7):
+            take(act, (t - 6) * half, (t - 6) * half, half)
+        if 8 <= t < 12:
+            if t == 8:
+                loads[1].wait()
+            project(0, count, True, t - 8, t - 7)
+        if t in (12, 13, 14, 15):
+            if t == 12:
+                loads[2].wait()
+                loads[3].wait()
+            own_pair(t - 12)
+
+    def drain(t):
+        if 16 <= t < 24:
+            dest[t - 16] = arrived(t - 16)
+            send_y(t - 16, dest.at[t - 16])
+        if 20 <= t < 28:
+            k = t - 20
+            base[k] = swap_y(k, dest[k])
+            send_core(k, base.at[k])
+        if 22 <= t < 30:
+            k = t - 22
+            set_far(k, swap_core(k, base[k]))
 
     loads[0].wait()
     pl.semaphore_wait(barrier, len(peers))
-    for j in (4, 5, 2, 3, 6, 7):
+    for j in range(8, CHUNKS):
         send_core(j, act.at[pl.ds(j * rows, rows)])
     slot(0)
-    for j in (4, 5, 2, 3, 6, 7):
+    slot(1)
+    for j in range(8, CHUNKS):
         base[j] = swap_core(j, chunk(act, j))
-        if j >= 4:
-            send_y(j, base.at[j])
-        elif j == 3:
-            slot(1)
+        send_y(j, base.at[j])
     slot(2)
     slot(3)
-    take(act, 0, 0, count)
-    loads[1].wait()
-    got(0)
-    slot(4)
-    project(0, count, True)
-    loads[2].wait()
-    loads[3].wait()
-    got(1)
-    slot(5)
-    own_pairs(0, 2)
-    got(2)
-    slot(6)
-    own_pairs(2, 4)
-    for t in range(7, SLOTS):
+    for t in range(4, SLOTS):
         got(t - 4)
         slot(t)
-    got(12)
-    for k in range(2):
-        dest[k] = arrived(k)
-        send_y(k, dest.at[k])
-    got(13)
-    for k in range(2, 4):
-        dest[k] = arrived(k)
-        send_y(k, dest.at[k])
-    for k in range(2):
-        base[k] = swap_y(k, dest[k])
-        send_core(k, base.at[k])
-    for k in range(2, 4):
-        set_far(k, swap_y(k, dest[k]))
-    for k in range(2):
-        set_far(k, swap_core(k, base[k]))
+        drain(t - 4)
+        work(t)
+    got(28)
+    drain(28)
+    for k in range(8, 10):
+        set_far(k, arrived(k))
+    got(29)
+    drain(29)
+    for k in range(10, 12):
+        set_far(k, arrived(k))
     take(far, 0, count, half)
-    project(count, half, False)
-    got(14)
-    for k in range(4, 6):
-        set_far(k, arrived(k))
-    got(15)
-    for k in range(6, 8):
-        set_far(k, arrived(k))
+    project(count, half, False, 0, 4)
+    for t in (30, 31):
+        got(t)
+        for k in range(2 * t - 48, 2 * t - 46):
+            set_far(k, arrived(k))
     take(far, half, count + half, half)
-    project(count + half, half, False)
+    project(count + half, half, False, 0, 4)
 
     last = 2 * (x % 2) + ylo
     half_cp, ax_cp, ay_cp, by_cp, bx_cp, r_cp = {}, {}, {}, {}, {}, {}
@@ -333,19 +339,21 @@
     def pair_of(i):
         return (last + 1 + i) % 4
 
-    def pair_step(i):
+    def attend_step(i):
         far_part(pair_of(i), mask_ref, kv_hi, kv_lo, q_ref, d_ref, s_own, c_own, stats, s_far, c_far,
                  w_hi, w_lo, t_hi, t_lo, att, g_hi, g_lo)
-        value = nn_dot(at_hi[...], g_hi[...]) + nn_dot(at_hi[...], g_lo[...]) + nn_dot(at_lo[...], g_hi[...])
-        value = value.reshape(8, 2, 2, 2, 16, 256)
-        for c in range(2):
-            for kind in range(2):
-                for part in range(2):
-                    for yh in range(2):
-                        term[i, c, kind, part, yh] = value[:, yh, c, part, :, kind * 128:(kind + 1) * 128]
+
+    def term_half(i, c, into):
+        hi, lo = at_hi[c], at_lo[c]
+        value = nn_dot(hi, g_hi[...]) + nn_dot(hi, g_lo[...]) + nn_dot(lo, g_hi[...])
+        value = value.reshape(8, 2, 2, 16, 256)
+        for kind in range(2):
+            for part in range(2):
+                for yh in range(2):
+                    into[i, kind, part, yh] = value[:, yh, part, :, kind * 128:(kind + 1) * 128]
 
     def half_copy(i):
-        return remote(term.at[i, 1 - core], half_in.at[i], half_s.at[i], half_r.at[i], core_dev)
+        return remote(term.at[i], half_in.at[i], half_s.at[i], half_r.at[i], core_dev)
 
     def moves(i):
         pair = pair_of(i)
@@ -366,42 +374,51 @@
 
     def sum_step(i):
         half_copy(i).wait_recv()
-        total[i] = term[i, core] + half_in[i]
+        total[i] = total[i] + half_in[i]
         for condition, copy in moves(i):
             pl.when(condition)(copy.start)
 
     for i in range(4):
-        pair_step(i)
+        attend_step(i)
+        term_half(i, 1 - core, term)
         half_copy(i).start()
         if i > 0:
             sum_step(i - 1)
+        term_half(i, core, total)
     out_copy = pltpu.make_async_copy(att, att_hbm, load_s.at[4])
     out_copy.start()
     sum_step(3)
 
-    mine = x // 2
-    for yl in range(2):
-        i = (2 * (x % 2) + yl - last + 3) % 4
-        value = total[i, mine, 0]
+    def second_x(yl):
+        value = total[(2 * (x % 2) + yl - last + 3) % 4, x // 2, 0]
         for n in range(1, 4):
             remote(total.at[0, 0, 0], ax_in.at[n - 1, yl], ax_s.at[0, 0], ax_r.at[n - 1, yl], x_dev[n]).wait_recv()
             value = value + ax_in[n - 1, yl]
         for yh in range(2):
             ax_sum[yh * 2 + yl] = value[yh]
-    for n in range(1, 4):
-        ay_cp[n] = remote(ax_sum.at[(y + n) % 4], ay_in.at[n - 1], ay_s.at[n - 1], ay_r.at[n - 1], y_dev[n])
-        ay_cp[n].start()
-    for to_x in range(4):
-        i = (2 * (to_x % 2) + ylo - last + 3) % 4
-        value = total[i, to_x // 2, 1, yhi]
+
+    def second_y(to_x):
+        value = total[(2 * (to_x % 2) + ylo - last + 3) % 4, to_x // 2, 1, yhi]
         for n in range(1, 4):
             remote(total.at[0, 0, 1, 0], by_in.at[n - 1, to_x], by_s.at[0, 0, 0], by_r.at[n - 1, to_x],
                    y_dev[n]).wait_recv()
             value = value + by_in[n - 1, to_x]
         by_sum[to_x] = value
+
     for n in range(1, 4):
+        ay_cp[n] = remote(ax_sum.at[(y + n) % 4], ay_in.at[n - 1], ay_s.at[n - 1], ay_r.at[n - 1], y_dev[n])
         bx_cp[n] = remote(by_sum.at[(x + n) % 4], bx_in.at[n - 1], bx_s.at[n - 1], bx_r.at[n - 1], x_dev[n])
+    second_x(1 - ylo)
+    ay_cp[1].start()
+    ay_cp[3].start()
+    for n in (1, 3):
+        second_y((x + n) % 4)
         bx_cp[n].start()
+    second_x(ylo)
+    ay_cp[2].start()
+    second_y((x + 2) % 4)
+    bx_cp[2].start()
+    second_y(x)
     value = ax_sum[y]
     for n in range(1, 4):
         ay_cp[n].wait_recv()
@@ -451,13 +468,13 @@
         scratch_shapes=[
             f32(count, depth), f32(count, depth), f32(count, width), f32(count, width), f32(depth, 2 * width),
             f32(CHUNKS, rows, depth), f32(CHUNKS, rows, depth), f32(CHUNKS, rows, depth),
-            f32(2, SLOTS, rows, depth), f32(2, SLOTS, rows, depth), f32(4, rows, depth),
+            f32(2, SLOTS, rows, depth), f32(2, SLOTS, rows, depth), f32(CHUNKS // 2, rows, depth),
             b16(depth, 2 * width), b16(depth, 2 * width), b16(keys, depth), b16(keys, depth),
-            b16(depth, keys), b16(depth, keys), b16(keys, 2 * width), b16(keys, 2 * width),
+            b16(2, depth // 2, keys), b16(2, depth // 2, keys), b16(keys, 2 * width), b16(keys, 2 * width),
             b16(keys, 256), b16(keys, 256), f32(pairs, count, keys), f32(pairs, count, keys), f32(pairs, 8, keys),
             f32(count, keys), f32(count, keys), b16(keys, keys), b16(keys, keys), b16(keys, keys), b16(keys, keys),
             f32(count, width),
-            f32(4, 2, 2, 2, 2, 8, 16, 128), f32(4, 2, 2, 2, 8, 16, 128), f32(4, 2, 2, 2, 8, 16, 128),
+            f32(4, 2, 2, 2, 8, 16, 128), f32(4, 2, 2, 2, 8, 16, 128), f32(4, 2, 2, 2, 8, 16, 128),
             f32(3, 2, 2, 8, 16, 128), f32(4, 8, 16, 128), f32(3, 8, 16, 128),
             f32(3, 4, 8, 16, 128), f32(4, 8, 16, 128), f32(3, 8, 16, 128),
             f32(8, 2, 16, 128), f32(7, 2, 16, 128),

time: 112 us -> 96.6 us (0.86)
  Pallas kernels: 107 us -> 91.9 us
    pallas_call x1, Pallas kernels: 107 us -> 91.9 us  [run(): pl.pallas_call(kernel, out_shape=(jax.ShapeDtypeStruct((count, width), F3...]
where the time goes in v3:
time: 96.6 us; the launch traced here: 96.4 us
  Pallas kernels  91.9 us (95%)
  local copies, waits for them, and re-layouts  3.19 us (3%)
  between operations  1.29 us (1%)
    pallas_call x1, Pallas kernels, run(): pl.pallas_call(kernel, out_shape=(jax.ShapeDtypeStruct((count, width), F3...  91.9 us
    unnamed x2, local copies, waits for them, and re-layouts  3.19 us

profile of v3, /device:TPU:2, one launch (start us, length us, event | category | flops | bytes accessed | tf_op | source)
XLA Modules:
  0.0 96.4 jit_solution(13579881644465356126)
XLA Ops:
  1.3 91.9 %shard_map.77 = (f32[256,512]{1,0:T(8,128)}, f32[32,128]{1,0:T(8,128)}) custom-call(s32[1,1]{1,0:T(1,128)S(6)} %copy.10.partner_ref, s32[4,4]{1,0:T(4,128)} %bitcast.9, f32[256,1024]{1,0:T(8,128)} %bitcast.5, f32[256,512]{1,0:T(8,128)} %bitcast.6, f32[256,512]{1,0:T(8,128)} %bitcast.7, f32[1024,1024]{1,0:T(8,128)} %w_hbm.1), custom_call_target="tpu_custom_call" | custom-call | tf_op jit(solution)/shard_map/pallas_call | solution.py:463
  93.2 1.9 %copy.11 = f32[1,256,512]{2,1,0:T(8,128)} copy(f32[1,256,512]{2,1,0:T(8,128)} %bitcast.8) | data formatting | bytes 1048576
  95.0 1.3 %copy.12 = f32[32,128]{1,0:T(8,128)} copy(f32[32,128]{1,0:T(8,128)} %get-tuple-element.9) | data formatting | bytes 32768

commit v4 on v3

--- a/solution.py
+++ b/solution.py
@@ -55,7 +55,23 @@
 BLOCK = 64
 
 
-def own_part(pair, kv_hi, kv_lo, q_ref, d_ref, s_own, c_own, stats):
+def weigh(kv_hi, kv_lo, rows, at_v, w_hi, w_lo):
+    flip = lambda value: value.astype(F32).T.astype(BF16)
+    vt_h, vt_l = flip(kv_hi[rows, at_v]), flip(kv_lo[rows, at_v])
+    out = nn_dot(jnp.concatenate([vt_h, vt_l], axis=0), w_hi[rows, :])
+    return out[:128] + out[128:] + nn_dot(vt_h, w_lo[rows, :])
+
+
+def far_scores(pair, start, size, kv_hi, kv_lo, q_ref, d_ref, s_far, c_far):
+    count, half = q_ref.shape[0], kv_hi.shape[1] // 2
+    first = lax.broadcasted_iota(jnp.int32, (count, 128), 1) < 64
+    at, at_v = lanes_of(pair), lanes_of(pair, half)
+    rows, into = pl.ds(count + start, size), pl.ds(start, size)
+    s_far[pair, into, :] = scores(kv_hi, kv_lo, rows, at, *head_pair(q_ref[:, at] * 0.125, first))
+    c_far[pair, into, :] = scores(kv_hi, kv_lo, rows, at_v, *head_pair(d_ref[:, at], first))
+
+
+def own_part(pair, kv_hi, kv_lo, q_ref, d_ref, s_own, c_own, stats, o_own, w_hi, w_lo):
     count, half = q_ref.shape[0], kv_hi.shape[1] // 2
     first = lax.broadcasted_iota(jnp.int32, (count, 128), 1) < 64
     at, at_v = lanes_of(pair), lanes_of(pair, half)
@@ -72,14 +88,16 @@
         rows = pl.ds(b * BLOCK, BLOCK)
         raised = jnp.exp(s_own[pair, rows, :] - maximum)
         s_own[pair, rows, :] = raised
+        w_hi[rows, :], w_lo[rows, :] = split(raised)
         total = total + jnp.sum(raised, axis=0, keepdims=True)
         dots = dots + jnp.sum(raised * c_own[pair, rows, :], axis=0, keepdims=True)
     stats[pair, pl.ds(0, 1), :] = maximum
     stats[pair, pl.ds(1, 1), :] = total
     stats[pair, pl.ds(2, 1), :] = dots
-
-
-def far_part(pair, mask_ref, kv_hi, kv_lo, q_ref, d_ref, s_own, c_own, stats, s_far, c_far,
+    o_own[pair] = weigh(kv_hi, kv_lo, own, at_v, w_hi, w_lo)
+
+
+def far_part(pair, mask_ref, kv_hi, kv_lo, q_ref, d_ref, s_own, c_own, stats, s_far, c_far, o_own,
              w_hi, w_lo, t_hi, t_lo, att, g_hi, g_lo):
     count, half = q_ref.shape[0], kv_hi.shape[1] // 2
     first = lax.broadcasted_iota(jnp.int32, (count, 128), 1) < 64
@@ -87,8 +105,9 @@
     q_h, q_l = head_pair(q_ref[:, at] * 0.125, first)
     d_h, d_l = head_pair(d_ref[:, at], first)
     far = pl.ds(count, count)
-    s_far[...] = scores(kv_hi, kv_lo, far, at, q_h, q_l)
-    c_far[...] = scores(kv_hi, kv_lo, far, at_v, d_h, d_l)
+    late, into = pl.ds(count + count // 2, count // 2), pl.ds(count // 2, count // 2)
+    s_far[pair, into, :] = scores(kv_hi, kv_lo, late, at, q_h, q_l)
+    c_far[pair, into, :] = scores(kv_hi, kv_lo, late, at_v, d_h, d_l)
     lanes = lax.broadcasted_iota(jnp.int32, (1, 2 * count), 1) % count // BLOCK
     own_max = stats[pair, pl.ds(0, 1), :]
     maximum = own_max
@@ -97,18 +116,18 @@
         rows = pl.ds(b * BLOCK, BLOCK)
         seen = jnp.where(lanes == 0, mask_ref[0, b], jnp.where(lanes == 1, mask_ref[1, b], jnp.where(
             lanes == 2, mask_ref[2, b], mask_ref[3, b])))
-        piece = jnp.where(seen == 1, s_far[rows, :], MASKED)
-        s_far[rows, :] = piece
+        piece = jnp.where(seen == 1, s_far[pair, rows, :], MASKED)
+        s_far[pair, rows, :] = piece
         maximum = jnp.maximum(maximum, jnp.max(piece, axis=0, keepdims=True))
     shrink = jnp.exp(own_max - maximum)
     total = stats[pair, pl.ds(1, 1), :] * shrink
     dots = stats[pair, pl.ds(2, 1), :] * shrink
     for b in range(blocks):
         rows = pl.ds(b * BLOCK, BLOCK)
-        raised = jnp.exp(s_far[rows, :] - maximum)
-        s_far[rows, :] = raised
+        raised = jnp.exp(s_far[pair, rows, :] - maximum)
+        s_far[pair, rows, :] = raised
         total = total + jnp.sum(raised, axis=0, keepdims=True)
-        dots = dots + jnp.sum(raised * c_far[rows, :], axis=0, keepdims=True)
+        dots = dots + jnp.sum(raised * c_far[pair, rows, :], axis=0, keepdims=True)
     inverse = 1.0 / total
     row_dot = dots * inverse
     own_scale = shrink * inverse
@@ -118,9 +137,9 @@
         w_hi[rows, :], w_lo[rows, :] = split(weight)
         t_hi[rows, :], t_lo[rows, :] = split(weight * (c_own[pair, rows, :] - row_dot))
         lower = pl.ds(count + b * BLOCK, BLOCK)
-        weight = s_far[rows, :] * inverse
+        weight = s_far[pair, rows, :] * inverse
         w_hi[lower, :], w_lo[lower, :] = split(weight)
-        t_hi[lower, :], t_lo[lower, :] = split(weight * (c_far[rows, :] - row_dot))
+        t_hi[lower, :], t_lo[lower, :] = split(weight * (c_far[pair, rows, :] - row_dot))
 
     def grads(left_hi, left_lo, right_h, right_l):
         both = nn_dot(left_hi[...], cat(right_h, right_l))
@@ -128,16 +147,13 @@
 
     g_hi[:, :128], g_lo[:, :128] = split(grads(t_hi, t_lo, q_h, q_l))
     g_hi[:, 128:], g_lo[:, 128:] = split(grads(w_hi, w_lo, d_h, d_l))
-    flip = lambda value: value.astype(F32).T.astype(BF16)
-    vt_h, vt_l = flip(kv_hi[:, at_v]), flip(kv_lo[:, at_v])
-    out = nn_dot(jnp.concatenate([vt_h, vt_l], axis=0), w_hi[...])
-    out = out[:128] + out[128:] + nn_dot(vt_h, w_lo[...])
+    out = o_own[pair] * own_scale + weigh(kv_hi, kv_lo, far, at_v, w_hi, w_lo)
     att[:, at] = jnp.concatenate([out[:64, :count], out[64:, count:]], axis=0).T
 
 
 def kernel(partner_ref, mask_ref, act_hbm, q_hbm, d_hbm, w_hbm, att_hbm, grad_ref,
            act, far, q_ref, d_ref, w_ref, core_in, base, y_in, z_out, z_in, dest,
-           p_hi, p_lo, a_hi, a_lo, at_hi, at_lo, kv_hi, kv_lo, g_hi, g_lo, s_own, c_own, stats, s_far, c_far,
+           p_hi, p_lo, a_hi, a_lo, at_hi, at_lo, kv_hi, kv_lo, g_hi, g_lo, s_own, c_own, stats, s_far, c_far, o_own,
            w_hi, w_lo, t_hi, t_lo, att,
            term, half_in, total, ax_in, ax_sum, ay_in, by_in, by_sum, bx_in, r_out, r_in,
            load_s, core_s, core_r, y_s, y_r, z_s, z_r,
@@ -264,14 +280,15 @@
                 p_hi[:, at], p_lo[:, at] = split(w_ref[:, at])
             rows_ = pl.ds(start, size)
             hi, lo = a_hi[rows_, :], a_lo[rows_, :]
-            pairs = nn_dot(hi, p_hi[:, at]) + nn_dot(hi, p_lo[:, at]) + nn_dot(lo, p_hi[:, at])
+            both = nn_dot(jnp.concatenate([hi, lo], axis=0), p_hi[:, at])
+            pairs = both[:size] + both[size:] + nn_dot(hi, p_lo[:, at])
             kv_hi[rows_, at], kv_lo[rows_, at] = split(pairs)
             return carry
         lax.fori_loop(n0, n1, step, 0)
 
     def own_pair(pair):
         def step(n, carry):
-            own_part(n, kv_hi, kv_lo, q_ref, d_ref, s_own, c_own, stats)
+            own_part(n, kv_hi, kv_lo, q_ref, d_ref, s_own, c_own, stats, o_own, w_hi, w_lo)
             return carry
         lax.fori_loop(pair, pair + 1, step, 0)
 
@@ -292,12 +309,12 @@
         if 16 <= t < 24:
             dest[t - 16] = arrived(t - 16)
             send_y(t - 16, dest.at[t - 16])
-        if 20 <= t < 28:
-            k = t - 20
+        if 19 <= t < 27:
+            k = t - 19
             base[k] = swap_y(k, dest[k])
             send_core(k, base.at[k])
-        if 22 <= t < 30:
-            k = t - 22
+        if 21 <= t < 29:
+            k = t - 21
             set_far(k, swap_core(k, base[k]))
 
     loads[0].wait()
@@ -318,15 +335,15 @@
         work(t)
     got(28)
     drain(28)
-    for k in range(8, 10):
-        set_far(k, arrived(k))
-    got(29)
-    drain(29)
-    for k in range(10, 12):
-        set_far(k, arrived(k))
     take(far, 0, count, half)
     project(count, half, False, 0, 4)
-    for t in (30, 31):
+
+    def early_scores(pair, carry):
+        far_scores(pair, 0, half, kv_hi, kv_lo, q_ref, d_ref, s_far, c_far)
+        return carry
+
+    lax.fori_loop(0, 4, early_scores, 0)
+    for t in range(28, 32):
         got(t)
         for k in range(2 * t - 48, 2 * t - 46):
             set_far(k, arrived(k))
@@ -340,7 +357,7 @@
         return (last + 1 + i) % 4
 
     def attend_step(i):
-        far_part(pair_of(i), mask_ref, kv_hi, kv_lo, q_ref, d_ref, s_own, c_own, stats, s_far, c_far,
+        far_part(pair_of(i), mask_ref, kv_hi, kv_lo, q_ref, d_ref, s_own, c_own, stats, s_far, c_far, o_own,
                  w_hi, w_lo, t_hi, t_lo, att, g_hi, g_lo)
 
     def term_half(i, c, into):
@@ -472,7 +489,7 @@
             b16(depth, 2 * width), b16(depth, 2 * width), b16(keys, depth), b16(keys, depth),
             b16(2, depth // 2, keys), b16(2, depth // 2, keys), b16(keys, 2 * width), b16(keys, 2 * width),
             b16(keys, 256), b16(keys, 256), f32(pairs, count, keys), f32(pairs, count, keys), f32(pairs, 8, keys),
-            f32(count, keys), f32(count, keys), b16(keys, keys), b16(keys, keys), b16(keys, keys), b16(keys, keys),
+            f32(pairs, count, keys), f32(pairs, count, keys), f32(pairs, 128, keys), b16(keys, keys), b16(keys, keys), b16(keys, keys), b16(keys, keys),
             f32(count, width),
             f32(4, 2, 2, 2, 8, 16, 128), f32(4, 2, 2, 2, 8, 16, 128), f32(4, 2, 2, 2, 8, 16, 128),
             f32(3, 2, 2, 8, 16, 128), f32(4, 8, 16, 128), f32(3, 8, 16, 128),

time: 96.6 us -> 95.5 us (0.989)
  Pallas kernels: 91.9 us -> 90.9 us
    pallas_call x1, Pallas kernels: 91.9 us -> 90.9 us  [run(): pl.pallas_call(kernel, out_shape=(jax.ShapeDtypeStruct((count, width), F3...]
where the time goes in v4:
time: 95.5 us; the launch traced here: 95.3 us
  Pallas kernels  90.9 us (95%)
  local copies, waits for them, and re-layouts  3.19 us (3%)
  between operations  1.29 us (1%)
    pallas_call x1, Pallas kernels, run(): pl.pallas_call(kernel, out_shape=(jax.ShapeDtypeStruct((count, width), F3...  90.9 us
    unnamed x2, local copies, waits for them, and re-layouts  3.19 us

profile of v4, /device:TPU:2, one launch (start us, length us, event | category | flops | bytes accessed | tf_op | source)
XLA Modules:
  0.0 95.3 jit_solution(800714492603272226)
XLA Ops:
  1.3 90.9 %shard_map.77 = (f32[256,512]{1,0:T(8,128)}, f32[32,128]{1,0:T(8,128)}) custom-call(s32[1,1]{1,0:T(1,128)S(6)} %copy.10.partner_ref, s32[4,4]{1,0:T(4,128)} %bitcast.9, f32[256,1024]{1,0:T(8,128)} %bitcast.5, f32[256,512]{1,0:T(8,128)} %bitcast.6, f32[256,512]{1,0:T(8,128)} %bitcast.7, f32[1024,1024]{1,0:T(8,128)} %w_hbm.1), custom_call_target="tpu_custom_call" | custom-call | tf_op jit(solution)/shard_map/pallas_call | solution.py:480
  92.1 1.9 %copy.11 = f32[1,256,512]{2,1,0:T(8,128)} copy(f32[1,256,512]{2,1,0:T(8,128)} %bitcast.8) | data formatting | bytes 1048576
  94.0 1.3 %copy.12 = f32[32,128]{1,0:T(8,128)} copy(f32[32,128]{1,0:T(8,128)} %get-tuple-element.9) | data formatting | bytes 32768

commit v5 on v4

--- a/solution.py
+++ b/solution.py
@@ -502,8 +502,41 @@
     )(partner, mask, act, queries, cotangent, w_kv)
 
 
+def hand_over_kernel(att_in, grad_in, att_out, grad_out, att_mid, grad_mid, in_s, out_s):
+    rows = att_mid.shape[1]
+    steps = [(grad_in, grad_mid, grad_out)]
+    for n in range(att_mid.shape[0]):
+        part = pl.ds(n * rows, rows)
+        steps.append((att_in.at[part], att_mid.at[n], att_out.at[part]))
+    inward = [pltpu.make_async_copy(src, mid, in_s.at[n]) for n, (src, mid, _) in enumerate(steps)]
+    outward = [pltpu.make_async_copy(mid, dst, out_s.at[n]) for n, (_, mid, dst) in enumerate(steps)]
+    for copy in inward:
+        copy.start()
+    for first, second in zip(inward, outward):
+        first.wait()
+        second.start()
+    for copy in outward:
+        copy.wait()
+
+
+def hand_over(attended, gradient):
+    anywhere = pl.BlockSpec(memory_space=pl.ANY)
+    count, width = attended.shape
+    return pl.pallas_call(
+        hand_over_kernel,
+        out_shape=(jax.ShapeDtypeStruct(attended.shape, F32), jax.ShapeDtypeStruct(gradient.shape, F32)),
+        in_specs=[anywhere, anywhere],
+        out_specs=(anywhere, anywhere),
+        scratch_shapes=[
+            pltpu.VMEM((4, count // 4, width), F32), pltpu.VMEM(gradient.shape, F32),
+            pltpu.SemaphoreType.DMA((5,)), pltpu.SemaphoreType.DMA((5,)),
+        ],
+    )(attended, gradient)
+
+
 def shards(activations, queries, d_out, w_kv, partner, block_mask):
     attended, gradient = run(activations[0], queries[0], d_out[0], w_kv, partner, block_mask[0, 0])
+    attended, gradient = hand_over(attended, gradient)
     return attended[None], gradient
 
 

time: 95.5 us -> 94.4 us (0.988)
  local copies, waits for them, and re-layouts: 3.19 us -> 0 us
  Pallas kernels: 90.9 us -> 92.7 us
    unnamed x2 -> x0, local copies, waits for them, and re-layouts: 3.19 us -> none
    pallas_call x0 -> x1, Pallas kernels: none -> 1.85 us  [hand_over(): pl.pallas_call(hand_over_kernel, out_shape=(jax.ShapeDtypeStruct(attended...]
where the time goes in v5:
time: 94.4 us; the launch traced here: 94.2 us
  Pallas kernels  92.7 us (98%)
  between operations  1.45 us (2%)
    pallas_call x1, Pallas kernels, run(): pl.pallas_call(kernel, out_shape=(jax.ShapeDtypeStruct((count, width), F3...  90.9 us

profile of v5, /device:TPU:2, one launch (start us, length us, event | category | flops | bytes accessed | tf_op | source)
XLA Modules:
  0.0 94.2 jit_solution(12422191959996716356)
XLA Ops:
  1.3 90.9 %shard_map.77 = (f32[256,512]{1,0:T(8,128)}, f32[32,128]{1,0:T(8,128)}) custom-call(s32[1,1]{1,0:T(1,128)S(6)} %copy.8.partner_ref, s32[4,4]{1,0:T(4,128)} %bitcast.8, f32[256,1024]{1,0:T(8,128)} %bitcast.5, f32[256,512]{1,0:T(8,128)} %bitcast.6, f32[256,512]{1,0:T(8,128)} %bitcast.7, f32[1024,1024]{1,0:T(8,128)} %w_hbm.1), custom_call_target="tpu_custom_call" | custom-call | tf_op jit(solution)/shard_map/pallas_call | solution.py:480
  92.1 1.9 %shard_map.78 = (f32[256,512]{1,0:T(8,128)}, f32[32,128]{1,0:T(8,128)}) custom-call(f32[256,512]{1,0:T(8,128)} %get-tuple-element.6.att_in, f32[32,128]{1,0:T(8,128)} %get-tuple-element.7.grad_in), custom_call_target="tpu_custom_call" | custom-call | tf_op jit(solution)/shard_map/pallas_call | solution.py:525
